TPU v7x, 32 devices: a whole 2x2x4 slice. The times are simulated.
32 devices in a mesh: img: 8 (over z, x), seq: 4 (over y, core).
Axes of the slice: x: 2, y: 2, z: 4, core: 2. Of those that a mesh axis runs over, the one named last changes fastest.
Arguments:
- media_tokens: bfloat16 [16, 576, 1024], P('img', 'seq'), may hold values from -6 to 6
- latents: bfloat16 [16, 64, 1024], P('img', 'seq'), may hold values from -6 to 6
- patch_count: int32 [16], P('img'), may hold values from 256 to 576, as said below
- w_query: bfloat16 [2, 1024, 512], P(None, ('img', 'seq')), may hold values from -0.1875 to 0.1875
- w_keyval: bfloat16 [2, 1024, 1024], P(None, ('img', 'seq')), may hold values from -0.1875 to 0.1875
- w_out: bfloat16 [2, 512, 1024], P(None, ('img', 'seq')), may hold values from -1 to 1
- w_up: bfloat16 [2, 1024, 4096], P(None, ('img', 'seq')), may hold values from -0.1875 to 0.1875
- w_down: bfloat16 [2, 4096, 1024], P(None, ('img', 'seq')), may hold values from -0.09375 to 0.09375
- norm_params: bfloat16 [2, 6, 1024], P(None, None, ('img', 'seq')), may hold values from -1.2 to 1.4, as said below
- cotangent: bfloat16 [16, 64, 1024], P('img', 'seq'), may hold values from -6 to 6
Outputs:
- latents_out: bfloat16 [16, 64, 1024], P('img', 'seq')
- grad_media: float32 [16, 576, 1024], P('img', 'seq')
- grad_latents: float32 [16, 64, 1024], P('img', 'seq')
- grad_query: float32 [2, 1024, 512], P(None, ('img', 'seq'))
- grad_keyval: float32 [2, 1024, 1024], P(None, ('img', 'seq'))
- grad_outproj: float32 [2, 512, 1024], P(None, ('img', 'seq'))
- grad_up: float32 [2, 1024, 4096], P(None, ('img', 'seq'))
- grad_down: float32 [2, 4096, 1024], P(None, ('img', 'seq'))
- grad_norms: float32 [2, 6, 1024], P(None, None, ('img', 'seq'))
Inputs may be any that keep to these rules, and one draw needn't show every extreme that they name: `patch_count`: each image has 256 or 576 live patches, the first ones of its slots; the images with 576 form one run of consecutive image numbers, wrapping around from the last to the first; some image has 576 and some 256. `norm_params`: gains in rows 0, 2 and 4, shifts in rows 1, 3 and 5.
All inputs are finite; a program needn't handle non-finite values.
Results may differ from a plain program's by a relative error of at most 0.025.
Values may be sent and summed in bfloat16 or wider, within the bound.
A program may use at most 192 MiB of HBM per device.

v0:
```python
import jax
import jax.numpy as jnp
from jax import lax
from jax.sharding import PartitionSpec as P

HEAD = 64


eps = 1e-05
highest = lax.Precision.HIGHEST


def norm_rows(values, gain, shift):
    centre = jnp.mean(values, axis=-1, keepdims=True)
    centred = values - centre
    spread = jnp.mean(centred * centred, axis=-1, keepdims=True)
    return centred * lax.rsqrt(spread + eps) * gain + shift


def exact_gelu(values):
    return jax.nn.gelu(values, approximate=False)


def project(left, right):
    return jnp.einsum("ird,de->ire", left, right, preferred_element_type=jnp.float32)


def project_back(grads, right):
    return jnp.einsum("ire,de->ird", grads, right, preferred_element_type=jnp.float32)


def weight_grad(left, grads):
    return jnp.einsum("ird,ire->de", left, grads, preferred_element_type=jnp.float32)


def split_heads(values):
    return values.reshape(values.shape[0], values.shape[1], -1, HEAD)


def attend_merge(scores, value_heads):
    local_top = jnp.max(scores, axis=-1, keepdims=True)
    row_top = lax.pmax(local_top, "seq")
    exp_scores = jnp.exp(scores - row_top)
    part_total = jnp.sum(exp_scores, axis=-1, keepdims=True)
    part_numer = jnp.einsum(
        "ihlk,ikhd->ihld",
        exp_scores.astype(jnp.bfloat16),
        value_heads,
        preferred_element_type=jnp.float32,
    )
    row_total, row_numer = (
        lax.psum(part_total.astype(jnp.bfloat16), "seq").astype(jnp.float32),
        lax.psum(part_numer.astype(jnp.bfloat16), "seq").astype(jnp.float32),
    )
    return (row_top, row_total, row_numer / row_total)


def layer_forward(current, media_tokens, valid_keys, weights):
    w_q, w_kv, w_o, w_u, w_d, normed = weights
    normed = normed.astype(jnp.float32)
    inner_width = w_q.shape[1]
    media_float = media_tokens.astype(jnp.float32)
    media_normed = norm_rows(media_float, normed[0], normed[1]).astype(jnp.bfloat16)
    media_kv = project(media_normed, w_kv).astype(jnp.bfloat16)
    latent_normed = norm_rows(current, normed[2], normed[3]).astype(jnp.bfloat16)
    latent_kv = project(latent_normed, w_kv).astype(jnp.bfloat16)
    gathered = lax.all_gather(latent_normed, "seq", axis=1, tiled=True)
    queries = project(gathered, w_q).astype(jnp.bfloat16)
    keys_all = jnp.concatenate([media_kv, latent_kv], axis=1)
    query_heads = split_heads(queries)
    key_heads = split_heads(keys_all[:, :, :inner_width])
    value_heads = split_heads(keys_all[:, :, inner_width:])
    live_keys = jnp.concatenate(
        [valid_keys, jnp.ones((valid_keys.shape[0], latent_kv.shape[1]), dtype=jnp.bool_)], axis=1
    )
    scores = (
        jnp.einsum("ilhd,ikhd->ihlk", query_heads, key_heads, preferred_element_type=jnp.float32)
        * 0.125
    )
    scores = jnp.where(live_keys[:, None, None, :], scores, -1000000000.0)
    row_top, row_total, attended_heads = attend_merge(scores, value_heads)
    attended_float = jnp.transpose(attended_heads, (0, 2, 1, 3)).reshape(queries.shape)
    own_count = current.shape[1]
    own_start = lax.axis_index("seq") * own_count
    own_attended = lax.dynamic_slice_in_dim(attended_float, own_start, own_count, 1).astype(
        jnp.bfloat16
    )
    after_attn = current + project(own_attended, w_o)
    ff_normed = norm_rows(after_attn, normed[4], normed[5]).astype(jnp.bfloat16)
    hidden_pre = project(ff_normed, w_u)
    activated = exact_gelu(hidden_pre).astype(jnp.bfloat16)
    result = after_attn + project(activated, w_d)
    kept_values = (
        media_float,
        media_normed,
        latent_normed,
        gathered,
        query_heads,
        key_heads,
        value_heads,
        scores,
        row_top,
        row_total,
        attended_float,
        own_attended,
        after_attn,
        ff_normed,
        hidden_pre,
        activated,
    )
    return (result, kept_values)


def layer_backward(current, media_tokens, valid_keys, weights, grad_result):
    w_q, w_kv, w_o, w_u, w_d, normed = weights
    normed = normed.astype(jnp.float32)
    inner_width = w_q.shape[1]
    result, kept_values = layer_forward(current, media_tokens, valid_keys, weights)
    (
        media_float,
        media_normed,
        latent_normed,
        gathered,
        query_heads,
        key_heads,
        value_heads,
        scores,
        row_top,
        row_total,
        attended_float,
        own_attended,
        after_attn,
        ff_normed,
        hidden_pre,
        activated,
    ) = kept_values
    grad_branch = grad_result.astype(jnp.bfloat16)
    g_down = weight_grad(activated, grad_branch)
    grad_act = jnp.einsum("ire,fe->irf", grad_branch, w_d, preferred_element_type=jnp.float32)
    gelu_value, gelu_pull = jax.vjp(exact_gelu, hidden_pre)
    grad_pre = gelu_pull(grad_act)[0].astype(jnp.bfloat16)
    g_up = weight_grad(ff_normed, grad_pre)
    grad_ffn = jnp.einsum("irf,df->ird", grad_pre, w_u, preferred_element_type=jnp.float32)
    ffn_value, ffn_pull = jax.vjp(norm_rows, after_attn, normed[4], normed[5])
    grad_after_norm, g_gain_ff, g_shift_ff = ffn_pull(grad_ffn)
    grad_after = grad_result + grad_after_norm
    grad_proj = grad_after.astype(jnp.bfloat16)
    g_out = weight_grad(own_attended, grad_proj)
    grad_own = project_back(grad_proj, w_o).astype(jnp.bfloat16)
    grad_attended = lax.all_gather(grad_own, "seq", axis=1, tiled=True)
    grad_heads = split_heads(grad_attended)
    attended_heads = split_heads(attended_float)
    grad_probs = jnp.einsum(
        "ilhd,ikhd->ihlk", grad_heads, value_heads, preferred_element_type=jnp.float32
    )
    row_delta = jnp.transpose(
        jnp.sum(grad_heads.astype(jnp.float32) * attended_heads, axis=-1), (0, 2, 1)
    )[..., None]
    exp_scores = jnp.exp(scores - row_top)
    grad_scores = (exp_scores / row_total * (grad_probs - row_delta)).astype(jnp.bfloat16)
    grad_query_part = (
        jnp.einsum("ihlk,ikhd->ilhd", grad_scores, key_heads, preferred_element_type=jnp.float32)
        * 0.125
    )
    query_shape = (gathered.shape[0], gathered.shape[1], inner_width)
    grad_query = lax.psum_scatter(
        grad_query_part.reshape(query_shape).astype(jnp.bfloat16),
        "seq",
        scatter_dimension=1,
        tiled=True,
    )
    grad_keys = (
        jnp.einsum("ihlk,ilhd->ikhd", grad_scores, query_heads, preferred_element_type=jnp.float32)
        * 0.125
    )
    weights_scaled = exp_scores.astype(jnp.bfloat16).astype(jnp.float32) / row_total
    grad_values = jnp.einsum(
        "ihlk,ilhd->ikhd", weights_scaled, grad_heads.astype(jnp.float32), precision=highest
    )
    key_count = grad_keys.shape[1]
    grad_kv = jnp.concatenate(
        [
            grad_keys.reshape(grad_keys.shape[0], key_count, inner_width),
            grad_values.reshape(grad_values.shape[0], key_count, inner_width),
        ],
        axis=2,
    ).astype(jnp.bfloat16)
    media_count = media_normed.shape[1]
    grad_media_kv = grad_kv[:, :media_count]
    grad_latent_kv = grad_kv[:, media_count:]
    g_query = weight_grad(latent_normed, grad_query)
    g_keyval = weight_grad(media_normed, grad_media_kv) + weight_grad(latent_normed, grad_latent_kv)
    grad_media_normed = project_back(grad_media_kv, w_kv)
    media_value, media_pull = jax.vjp(norm_rows, media_float, normed[0], normed[1])
    grad_media, g_gain_media, g_shift_media = media_pull(grad_media_normed)
    grad_latent_normed = project_back(grad_query, w_q) + project_back(grad_latent_kv, w_kv)
    latent_value, latent_pull = jax.vjp(norm_rows, current, normed[2], normed[3])
    grad_current, g_gain_latent, g_shift_latent = latent_pull(grad_latent_normed)
    grad_input = grad_after + grad_current
    g_norms = jnp.stack(
        [g_gain_media, g_shift_media, g_gain_latent, g_shift_latent, g_gain_ff, g_shift_ff], axis=0
    )
    return (grad_input, grad_media, (g_query, g_keyval, g_out, g_up, g_down, g_norms))


def reduce_weights(partials):
    return (
        lax.psum_scatter(partials[0], ("img", "seq"), scatter_dimension=0, tiled=True),
        lax.psum_scatter(partials[1], ("img", "seq"), scatter_dimension=0, tiled=True),
        lax.psum_scatter(partials[2], ("img", "seq"), scatter_dimension=0, tiled=True),
        lax.psum_scatter(partials[3], ("img", "seq"), scatter_dimension=0, tiled=True),
        lax.psum_scatter(partials[4], ("img", "seq"), scatter_dimension=0, tiled=True),
        lax.psum_scatter(partials[5], ("img", "seq"), scatter_dimension=1, tiled=True),
    )


def body(
    media_tokens,
    latents,
    patch_count,
    w_query,
    w_keyval,
    w_out,
    w_up,
    w_down,
    norm_params,
    cotangent,
):
    layer_total = w_query.shape[0]
    patch_rows = media_tokens.shape[1]
    positions = lax.axis_index("seq") * patch_rows + jnp.arange(patch_rows, dtype=jnp.int32)
    valid_keys = positions[None, :] < patch_count[:, None]
    gathered_weights = []
    for layer_id in range(layer_total):
        gathered_weights.append(
            (
                lax.all_gather(w_query[layer_id], ("img", "seq"), axis=0, tiled=True),
                lax.all_gather(w_keyval[layer_id], ("img", "seq"), axis=0, tiled=True),
                lax.all_gather(w_out[layer_id], ("img", "seq"), axis=0, tiled=True),
                lax.all_gather(w_up[layer_id], ("img", "seq"), axis=0, tiled=True),
                lax.all_gather(w_down[layer_id], ("img", "seq"), axis=0, tiled=True),
                lax.all_gather(norm_params[layer_id], ("img", "seq"), axis=1, tiled=True),
            )
        )
    layer_inputs = []
    current = latents.astype(jnp.float32)
    for layer_id in range(layer_total):
        layer_inputs.append(current)
        current, unused_values = layer_forward(
            current, media_tokens, valid_keys, gathered_weights[layer_id]
        )
    grad_current = cotangent.astype(jnp.float32)
    grad_media = jnp.zeros(media_tokens.shape, jnp.float32)
    reduced = [None] * layer_total
    for layer_id in reversed(range(layer_total)):
        grad_current, media_part, partials = layer_backward(
            layer_inputs[layer_id],
            media_tokens,
            valid_keys,
            gathered_weights[layer_id],
            grad_current,
        )
        grad_media = grad_media + media_part
        reduced[layer_id] = reduce_weights(partials)
    stacked = [
        jnp.stack([reduced[layer_id][member] for layer_id in range(layer_total)], axis=0)
        for member in range(6)
    ]
    return (
        current.astype(jnp.bfloat16),
        grad_media,
        grad_current,
        stacked[0],
        stacked[1],
        stacked[2],
        stacked[3],
        stacked[4],
        stacked[5],
    )


def solution(mesh):
    placed = (
        P("img", "seq", None),
        P("img", "seq", None),
        P("img"),
        P(None, ("img", "seq"), None),
        P(None, ("img", "seq"), None),
        P(None, ("img", "seq"), None),
        P(None, ("img", "seq"), None),
        P(None, ("img", "seq"), None),
        P(None, None, ("img", "seq")),
        P("img", "seq", None),
    )
    return jax.shard_map(
        body,
        mesh=mesh,
        in_specs=placed,
        out_specs=(
            P("img", "seq", None),
            P("img", "seq", None),
            P("img", "seq", None),
            P(None, ("img", "seq"), None),
            P(None, ("img", "seq"), None),
            P(None, ("img", "seq"), None),
            P(None, ("img", "seq"), None),
            P(None, ("img", "seq"), None),
            P(None, None, ("img", "seq")),
        ),
        check_vma=False,
    )
```

profile of v0, /device:TPU:9, one launch (start us, length us, event | category | flops | bytes accessed | tf_op | source)
XLA Modules:
  0.0 2689.8 jit_solution(631025222121148295)
XLA Ops:
  11.9 38.0 %all-gather = bf16[1,6,1024]{1,0,2:T(2,128)(2,1)S(1)} all-gather(bf16[1,6,32]{1,0,2:T(2,128)(2,1)S(1)} %copy.132), channel_id=2, replica_groups=mesh['img'=8,'seq'=4] {'img','seq'}, dimensions={2}, use_global_device_ids=true | all-gather | bytes 12672 | tf_op jit(solution)/shard_map/all_gather | solution.py:242
  77.5 47.3 %all-gather.25.cloned.1.call-done = bf16[1,1024,1024]{2,1,0:T(8,128)(2,1)} async-done(((bf16[1,32,1024]{2,1,0:T(8,128)(2,1)}), bf16[1,1024,1024]{2,1,0:T(8,128)(2,1)}) %all-gather.25.cloned.1.call-update) | async-done | bytes 2097168 | tf_op jit(solution)/shard_map/all_gather | solution.py:238
  140.7 37.6 %all-gather.6 = bf16[1,6,1024]{1,0,2:T(2,128)(2,1)S(1)} all-gather(bf16[1,6,32]{1,0,2:T(2,128)(2,1)S(1)} %copy.133), channel_id=8, replica_groups=mesh['img'=8,'seq'=4] {'img','seq'}, dimensions={2}, use_global_device_ids=true | all-gather | bytes 12672 | tf_op jit(solution)/shard_map/all_gather | solution.py:242
  178.8 17.3 slice_reduce_fusion.1
  218.8 56.7 %all-gather.27.cloned.1.call-done = bf16[1,512,1024]{2,1,0:T(8,128)(2,1)} async-done(((bf16[1,16,1024]{2,1,0:T(8,128)(2,1)}), bf16[1,512,1024]{2,1,0:T(8,128)(2,1)}) %all-gather.27.cloned.1.call-update) | async-done | bytes 1048592 | tf_op jit(solution)/shard_map/all_gather | solution.py:239
  277.3 78.7 %all-gather.29.cloned.1.call-done = bf16[1,1024,4096]{2,1,0:T(8,128)(2,1)} async-done(((bf16[1,32,4096]{2,1,0:T(8,128)(2,1)}), bf16[1,1024,4096]{2,1,0:T(8,128)(2,1)}) %all-gather.29.cloned.1.call-update) | async-done | bytes 8388624 | tf_op jit(solution)/shard_map/all_gather | solution.py:240
  361.1 74.9 %all-gather.31.cloned.1.call-done = bf16[1,4096,1024]{2,1,0:T(8,128)(2,1)} async-done(((bf16[1,128,1024]{2,1,0:T(8,128)(2,1)}), bf16[1,4096,1024]{2,1,0:T(8,128)(2,1)}) %all-gather.31.cloned.1.call-update) | async-done | bytes 8388624 | tf_op jit(solution)/shard_map/all_gather | solution.py:241
  450.9 40.5 %all-gather.33.cloned.1.call-done = bf16[1,1024,512]{2,1,0:T(8,128)(2,1)} async-done(((bf16[1,32,512]{2,1,0:T(8,128)(2,1)}), bf16[1,1024,512]{2,1,0:T(8,128)(2,1)}) %all-gather.33.cloned.1.call-update) | async-done | bytes 1048592 | tf_op jit(solution)/shard_map/all_gather | solution.py:237
  513.6 22.1 all-reduce.6.cloned.1.call-done
  539.5 54.0 %all-gather.37.cloned.1.call-done = bf16[1,512,1024]{2,1,0:T(8,128)(2,1)} async-done(((bf16[1,16,1024]{2,1,0:T(8,128)(2,1)}), bf16[1,512,1024]{2,1,0:T(8,128)(2,1)}) %all-gather.37.cloned.1.call-update) | async-done | bytes 1048592 | tf_op jit(solution)/shard_map/all_gather | solution.py:239
  597.0 76.7 %all-gather.39.cloned.1.call-done = bf16[1,1024,4096]{2,1,0:T(8,128)(2,1)} async-done(((bf16[1,32,4096]{2,1,0:T(8,128)(2,1)}), bf16[1,1024,4096]{2,1,0:T(8,128)(2,1)}) %all-gather.39.cloned.1.call-update) | async-done | bytes 8388624 | tf_op jit(solution)/shard_map/all_gather | solution.py:240
  680.2 72.3 %all-gather.41.cloned.1.call-done = bf16[1,4096,1024]{2,1,0:T(8,128)(2,1)} async-done(((bf16[1,128,1024]{2,1,0:T(8,128)(2,1)}), bf16[1,4096,1024]{2,1,0:T(8,128)(2,1)}) %all-gather.41.cloned.1.call-update) | async-done | bytes 8388624 | tf_op jit(solution)/shard_map/all_gather | solution.py:241
  919.8 42.4 %reduce-scatter.45.cloned.1.call-done = f32[32,6]{1,0:T(8,128)} async-done(((f32[1024,6]{1,0:T(8,128)}), f32[32,6]{1,0:T(8,128)}) %reduce-scatter.45.cloned.1.call-update) | async-done | bytes 784
  963.9 130.9 %reduce-scatter.43.cloned.1.call-done = f32[32,6]{1,0:T(8,128)} async-done(((f32[1024,6]{1,0:T(8,128)}), f32[32,6]{1,0:T(8,128)}) %reduce-scatter.43.cloned.1.call-update) | async-done | bytes 784
  1096.2 132.9 %reduce-scatter.33.cloned.1.call-done = f32[16,1024]{1,0:T(8,128)} async-done(((f32[512,1024]{1,0:T(8,128)}), f32[16,1024]{1,0:T(8,128)}) %reduce-scatter.33.cloned.1.call-update) | async-done | bytes 65552 | tf_op jit(solution)/shard_map/reduce_scatter | solution.py:210
  1229.0 134.8 %reduce-scatter.31.cloned.1.call-done = f32[16,1024]{1,0:T(8,128)} async-done(((f32[512,1024]{1,0:T(8,128)}), f32[16,1024]{1,0:T(8,128)}) %reduce-scatter.31.cloned.1.call-update) | async-done | bytes 65552 | tf_op jit(solution)/shard_map/reduce_scatter | solution.py:210
  1365.3 133.4 %reduce-scatter.25.cloned.1.call-done = f32[32,512]{1,0:T(8,128)} async-done(((f32[1024,512]{1,0:T(8,128)}), f32[32,512]{1,0:T(8,128)}) %reduce-scatter.25.cloned.1.call-update) | async-done | bytes 65552 | tf_op jit(solution)/shard_map/reduce_scatter | solution.py:208
  1498.7 134.8 %reduce-scatter.23.cloned.1.call-done = f32[32,512]{1,0:T(8,128)} async-done(((f32[1024,512]{1,0:T(8,128)}), f32[32,512]{1,0:T(8,128)}) %reduce-scatter.23.cloned.1.call-update) | async-done | bytes 65552 | tf_op jit(solution)/shard_map/reduce_scatter | solution.py:208
  1635.0 137.5 %reduce-scatter.29.cloned.1.call-done = f32[32,1024]{1,0:T(8,128)} async-done(((f32[1024,1024]{1,0:T(8,128)}), f32[32,1024]{1,0:T(8,128)}) %reduce-scatter.29.cloned.1.call-update) | async-done | bytes 131088 | tf_op jit(solution)/shard_map/reduce_scatter | solution.py:209
  1772.5 139.3 %reduce-scatter.27.cloned.1.call-done = f32[32,1024]{1,0:T(8,128)} async-done(((f32[1024,1024]{1,0:T(8,128)}), f32[32,1024]{1,0:T(8,128)}) %reduce-scatter.27.cloned.1.call-update) | async-done | bytes 131088 | tf_op jit(solution)/shard_map/reduce_scatter | solution.py:209
  1913.5 206.6 %reduce-scatter.41.cloned.1.call-done = f32[128,1024]{1,0:T(8,128)} async-done(((f32[4096,1024]{1,0:T(8,128)}), f32[128,1024]{1,0:T(8,128)}) %reduce-scatter.41.cloned.1.call-update) | async-done | bytes 524304 | tf_op jit(solution)/shard_map/reduce_scatter | solution.py:212
  2120.2 186.8 %reduce-scatter.39.cloned.1.call-done = f32[128,1024]{1,0:T(8,128)} async-done(((f32[4096,1024]{1,0:T(8,128)}), f32[128,1024]{1,0:T(8,128)}) %reduce-scatter.39.cloned.1.call-update) | async-done | bytes 524304 | tf_op jit(solution)/shard_map/reduce_scatter | solution.py:212
  2309.2 184.6 %reduce-scatter.37.cloned.1.call-done = f32[32,4096]{1,0:T(8,128)} async-done(((f32[1024,4096]{1,0:T(8,128)}), f32[32,4096]{1,0:T(8,128)}) %reduce-scatter.37.cloned.1.call-update) | async-done | bytes 524304 | tf_op jit(solution)/shard_map/reduce_scatter | solution.py:211
  2493.8 186.8 %reduce-scatter.35.cloned.1.call-done = f32[32,4096]{1,0:T(8,128)} async-done(((f32[1024,4096]{1,0:T(8,128)}), f32[32,4096]{1,0:T(8,128)}) %reduce-scatter.35.cloned.1.call-update) | async-done | bytes 524304 | tf_op jit(solution)/shard_map/reduce_scatter | solution.py:211
  (523 shorter events, 306.8 us)
Async XLA Ops:
  8.7 116.1 %all-gather.25.cloned.1.call-start = ((), (), s32[]{:S(2)}) async-start(), calls=%async_computation.29 | async-start | bytes 2162688 | tf_op jit(solution)/shard_map/all_gather | solution.py:238
  10.3 191.7 %all-gather.35.cloned.1.call-start = ((), (), s32[]{:S(2)}) async-start(), calls=%async_computation.34 | async-start | bytes 2162688 | tf_op jit(solution)/shard_map/all_gather | solution.py:238
  11.0 206.3 %all-reduce.4.cloned.1.call-start = ((), (), s32[]{:S(2)}) async-start(), calls=%async_computation.14 | async-start | bytes 524288 | tf_op jit(solution)/shard_map/psum | solution.py:53
  136.4 139.1 %all-gather.27.cloned.1.call-start = ((), (), s32[]{:S(2)}) async-start(), calls=%async_computation.30 | async-start | bytes 1081344 | tf_op jit(solution)/shard_map/all_gather | solution.py:239
  137.9 218.0 %all-gather.29.cloned.1.call-start = ((), (), s32[]{:S(2)}) async-start(), calls=%async_computation.31 | async-start | bytes 8650752 | tf_op jit(solution)/shard_map/all_gather | solution.py:240
  138.9 297.1 %all-gather.31.cloned.1.call-start = ((), (), s32[]{:S(2)}) async-start(), calls=%async_computation.32 | async-start | bytes 8650752 | tf_op jit(solution)/shard_map/all_gather | solution.py:241
  139.8 351.6 %all-gather.33.cloned.1.call-start = ((), (), s32[]{:S(2)}) async-start(), calls=%async_computation.33 | async-start | bytes 1081344 | tf_op jit(solution)/shard_map/all_gather | solution.py:237
  140.5 395.1 %all-reduce.6.cloned.1.call-start = ((), (), s32[]{:S(2)}) async-start(), calls=%async_computation.15 | async-start | bytes 524288 | tf_op jit(solution)/shard_map/psum | solution.py:53
  503.8 89.7 %all-gather.37.cloned.1.call-start = ((), (), s32[]{:S(2)}) async-start(), calls=%async_computation.35 | async-start | bytes 1081344 | tf_op jit(solution)/shard_map/all_gather | solution.py:239
  504.3 169.3 %all-gather.39.cloned.1.call-start = ((), (), s32[]{:S(2)}) async-start(), calls=%async_computation.36 | async-start | bytes 8650752 | tf_op jit(solution)/shard_map/all_gather | solution.py:240
  505.1 247.5 %all-gather.41.cloned.1.call-start = ((), (), s32[]{:S(2)}) async-start(), calls=%async_computation.37 | async-start | bytes 8650752 | tf_op jit(solution)/shard_map/all_gather | solution.py:241
  505.7 292.3 %reduce-scatter.19.cloned.1.call-start = ((), (), s32[]{:S(2)}) async-start(), calls=%async_computation.16 | async-start | bytes 163840 | tf_op jit(solution)/shard_map/reduce_scatter | solution.py:166
  830.4 131.9 %reduce-scatter.45.cloned.1.call-start = ((), (), s32[]{:S(2)}) async-start(), calls=%async_computation.39 | async-start | bytes 540672
  837.6 257.1 %reduce-scatter.43.cloned.1.call-start = ((), (), s32[]{:S(2)}) async-start(), calls=%async_computation.38 | async-start | bytes 540672
  852.2 376.9 %reduce-scatter.33.cloned.1.call-start = ((), (), s32[]{:S(2)}) async-start(), calls=%async_computation.23 | async-start | bytes 2162688 | tf_op jit(solution)/shard_map/reduce_scatter | solution.py:210
  854.9 509.0 %reduce-scatter.31.cloned.1.call-start = ((), (), s32[]{:S(2)}) async-start(), calls=%async_computation.22 | async-start | bytes 2162688 | tf_op jit(solution)/shard_map/reduce_scatter | solution.py:210
  858.3 640.5 %reduce-scatter.25.cloned.1.call-start = ((), (), s32[]{:S(2)}) async-start(), calls=%async_computation.19 | async-start | bytes 2162688 | tf_op jit(solution)/shard_map/reduce_scatter | solution.py:208
  860.9 772.6 %reduce-scatter.23.cloned.1.call-start = ((), (), s32[]{:S(2)}) async-start(), calls=%async_computation.18 | async-start | bytes 2162688 | tf_op jit(solution)/shard_map/reduce_scatter | solution.py:208
  863.6 908.9 %reduce-scatter.29.cloned.1.call-start = ((), (), s32[]{:S(2)}) async-start(), calls=%async_computation.21 | async-start | bytes 4325376 | tf_op jit(solution)/shard_map/reduce_scatter | solution.py:209
  868.8 1043.1 %reduce-scatter.27.cloned.1.call-start = ((), (), s32[]{:S(2)}) async-start(), calls=%async_computation.20 | async-start | bytes 4325376 | tf_op jit(solution)/shard_map/reduce_scatter | solution.py:209
  874.0 1246.2 %reduce-scatter.41.cloned.1.call-start = ((), (), s32[]{:S(2)}) async-start(), calls=%async_computation.27 | async-start | bytes 17301504 | tf_op jit(solution)/shard_map/reduce_scatter | solution.py:212
  883.5 1423.4 %reduce-scatter.39.cloned.1.call-start = ((), (), s32[]{:S(2)}) async-start(), calls=%async_computation.26 | async-start | bytes 17301504 | tf_op jit(solution)/shard_map/reduce_scatter | solution.py:212
  893.1 1600.7 %reduce-scatter.37.cloned.1.call-start = ((), (), s32[]{:S(2)}) async-start(), calls=%async_computation.25 | async-start | bytes 17301504 | tf_op jit(solution)/shard_map/reduce_scatter | solution.py:211
  902.3 1778.3 %reduce-scatter.35.cloned.1.call-start = ((), (), s32[]{:S(2)}) async-start(), calls=%async_computation.24 | async-start | bytes 17301504 | tf_op jit(solution)/shard_map/reduce_scatter | solution.py:211
  (158 other events, 2388.1 us)
Sparse Core Ops, SparseCore 0:
  11.5 54.6 all-gather.22
  69.6 55.1 all-gather.24
  128.2 55.4 all-gather.34
  186.5 30.7 all-reduce.3
  221.0 54.4 all-gather.26
  278.6 77.2 all-gather.28
  359.8 76.1 all-gather.30
  439.8 51.4 all-gather.32
  503.9 31.7 all-reduce.5
  539.0 54.4 all-gather.36
  596.4 77.2 all-gather.38
  676.4 76.1 all-gather.40
  851.7 110.4 reduce-scatter.44
  965.0 129.6 reduce-scatter.42
  1096.9 132.1 reduce-scatter.32
  1231.2 132.5 reduce-scatter.30
  1366.1 132.6 reduce-scatter.24
  1500.9 132.5 reduce-scatter.22
  1635.8 136.7 reduce-scatter.28
  1774.8 136.9 reduce-scatter.26
  1914.1 205.9 reduce-scatter.40
  2122.3 184.5 reduce-scatter.38
  2309.2 184.5 reduce-scatter.36
  2496.0 184.5 reduce-scatter.34
  (2 shorter events, 35.6 us)
where the time goes:
time: 2700 us; the launch traced here: 2690 us
  waiting for transfers between devices  2310 us (86%)
  matrix products  135 us (5%)
  blocking collectives  123 us (5%)
  local copies, waits for them, and re-layouts  76.4 us (3%)
    reduce_scatter x2, waiting for transfers between devices, reduce_weights(): lax.psum_scatter(partials[4], ('img', 'seq'), scatter_dimension=0, tiled=...  393 us
    reduce_scatter x2, waiting for transfers between devices, reduce_weights(): lax.psum_scatter(partials[3], ('img', 'seq'), scatter_dimension=0, tiled=...  371 us
    reduce_scatter x2, waiting for transfers between devices, reduce_weights(): lax.psum_scatter(partials[1], ('img', 'seq'), scatter_dimension=0, tiled=...  277 us
    reduce_scatter x2, waiting for transfers between devices, reduce_weights(): lax.psum_scatter(partials[0], ('img', 'seq'), scatter_dimension=0, tiled=...  268 us
    reduce_scatter x2, waiting for transfers between devices, reduce_weights(): lax.psum_scatter(partials[2], ('img', 'seq'), scatter_dimension=0, tiled=...  268 us
    unnamed x28, waiting for transfers between devices  177 us
    all_gather x2, waiting for transfers between devices, body(): lax.all_gather(w_up[layer_id], ('img', 'seq'), axis=0, tiled=True)  155 us
    all_gather x2, waiting for transfers between devices, body(): lax.all_gather(w_down[layer_id], ('img', 'seq'), axis=0, tiled=True)  147 us
  transfers between devices with their start and end apart: 26, of which 24 were waited for; matrix products, arithmetic and copies ran while one was open for 6% of the time, Pallas kernels for 0%

commit v1 on v0

v1 whole, which is shorter than its diff:
```python
import functools

import jax
import jax.numpy as jnp
from jax import lax
from jax.experimental import pallas as pl
from jax.experimental.pallas import tpu as pltpu
from jax.sharding import PartitionSpec as P

HEAD = 64
EPS = 1e-05
MESH = pl.DeviceIdType.MESH
BF = jnp.bfloat16
F32 = jnp.float32
TP = 8


class Sizes:
    def __init__(self, mesh, media, latents, wq, wkv, wout, wup, wdown):
        self.ni, self.ns = mesh.shape["img"], mesh.shape["seq"]
        self.ny = self.ns // 2
        self.chips = self.ni * self.ny
        self.layers = wq.shape[0]
        self.d = media.shape[2]
        self.nimg, self.pr = media.shape[0], media.shape[1]
        self.lr = latents.shape[1]
        self.inner = wq.shape[2]
        self.half = self.inner // 2
        self.ff = wup.shape[2]
        self.fs = self.ff // TP
        self.dp = self.chips // TP
        self.fc = self.ff // self.chips
        self.pm = self.pr * self.ns
        self.latn = self.lr * self.ns
        self.r = self.latn // 2
        self.keys = self.pm + self.latn
        self.heads = self.half // HEAD
        self.rows = TP * self.r
        self.mt = BF if self.pr % 16 == 0 else F32
        self.lt = BF if self.lr % 16 == 0 else F32
        assert self.nimg == self.ny and TP % self.ny == 0


def dot(a, b, ca=1, cb=0):
    return lax.dot_general(a, b, (((ca,), (cb,)), ((), ())), preferred_element_type=F32)


def centre(v):
    c = v - jnp.mean(v, axis=-1, keepdims=True)
    rstd = lax.rsqrt(jnp.mean(c * c, axis=-1, keepdims=True) + EPS)
    return c * rstd, rstd


def pull(xhat, rstd, cot, gain):
    g = cot * gain
    m1 = jnp.mean(g, axis=-1, keepdims=True)
    m2 = jnp.mean(g * xhat, axis=-1, keepdims=True)
    return rstd * (g - m1 - xhat * m2)


def col_sum(v):
    return jnp.sum(v, axis=0, keepdims=True)


def kernel(z, media_in, latcot_in, counts, nrm_in, wqkv_in, wo_in, wup_in, wdn_in,
           lat_out, gmedia_out, glat_out, gqkv, gout, gup, gdn, gn_out,
           media, lc, mn, kv, wqkv, wo, wup, wdn, nrm, q4, pexp, rtot, att4, atta, aft,
           ffa, hp, act, xs, gza, psend, precv, gpre, gya, gl, grecv, gkvm, macc, msend, mrecv, gn, xout, gxo, cm, fold,
           ss, rs, ls):
    L = z.layers
    i = lax.axis_index("img")
    s = lax.axis_index("seq")
    y, c = s // 2, s % 2
    k = i * z.ny + y
    pos, grp = k % TP, k // TP
    sib = (i, y * 2 + (1 - c))

    def chip(kk, cc):
        return (kk // z.ny, (kk % z.ny) * 2 + cc)

    def peer(t):
        return chip(grp * TP + (pos + t) % TP, c)

    waits = []
    count = [0]

    def sem():
        count[0] += 1
        return count[0] - 1

    def send(src, dst, dev, n):
        pltpu.make_async_remote_copy(src, dst, ss.at[n], rs.at[n], device_id=dev, device_id_type=MESH).start()

    def arrive(ref, n):
        pltpu.make_async_copy(ref, ref, rs.at[n]).wait()

    def local(src, dst, n):
        pltpu.make_async_copy(src, dst, ls.at[n]).start()

    def landed(src, dst, n):
        pltpu.make_async_copy(src, dst, ls.at[n]).wait()

    def sent(ref, n):
        waits.append((ref, n))

    bar = pltpu.get_barrier_semaphore()
    total = z.ni * z.ns
    me = i * z.ns + s

    def greet(t, _):
        o = (me + t) % total
        pl.semaphore_signal(bar, inc=1, device_id=(o // z.ns, o % z.ns), device_id_type=MESH)
        return 0

    lax.fori_loop(1, total, greet, 0)
    pl.semaphore_wait(bar, total - 1)

    loads = [(nrm_in, nrm), (wqkv_in.at[0], wqkv.at[0]), (wo_in.at[0], wo.at[0]), (wup_in.at[0], wup.at[0]),
             (wdn_in.at[0], wdn.at[0]), (wqkv_in.at[1], wqkv.at[1]), (wo_in.at[1], wo.at[1]),
             (wup_in.at[1], wup.at[1]), (wdn_in.at[1], wdn.at[1])]

    n_lc, n_ma, n_mb = sem(), sem(), sem()
    own_slot = s % z.ny
    for yy in range(z.ny):
        to = yy * 2 + s // z.ny

        @pl.when(to != s)
        def _():
            send(latcot_in.at[yy], lc.at[own_slot], (i, to), n_lc)

        @pl.when(to == s)
        def _():
            pltpu.make_async_copy(latcot_in.at[yy], lc.at[own_slot], rs.at[n_lc]).start()

    for t in range(1, z.ny):
        yy = (y + t) % z.ny
        send(media_in.at[yy], media.at[s], (i, yy * 2 + c), n_ma)
    pltpu.make_async_copy(media_in.at[y], media.at[s], rs.at[n_ma]).start()
    send(media_in.at[y], media.at[s], sib, n_mb)
    for n, (a, b) in enumerate(loads):
        local(a, b, n)
    arrive(lc, n_lc)
    cot = lc[:, 1].astype(F32).reshape(z.r, z.d)
    xs[0] = lc[:, 0].astype(F32).reshape(z.r, z.d)

    n_ff = [sem() for _ in range(L)]
    n_gz = [sem() for _ in range(L)]
    n_rs = [sem() for _ in range(2 * L)]
    n_ln = [sem() for _ in range(L)]
    n_at = [sem() for _ in range(L)]
    n_gy = [sem() for _ in range(L)]
    n_gl = [sem() for _ in range(L)]
    n_md = sem()
    n_lo, n_go, n_mo = sem(), sem(), sem()

    def gather_start(buf, value, n):
        buf[pos] = value
        for t in range(1, TP):
            send(buf.at[pos], buf.at[pos], peer(t), n)

    def gather_end(buf, n):
        arrive(buf.at[pl.ds(0, TP - 1)], n)
        sent(buf.at[pl.ds(0, TP - 1)], n)

    def swap(ref, value, n):
        ref[...] = value
        send(ref, ref, sib, n)
        arrive(ref, n)
        sent(ref, n)

    def pair_swap(buf, value, n):
        swap(buf.at[c], value, n)

    def scatter_sum(part, j):
        n = n_rs[j]
        psend[j] = part.astype(BF).reshape(TP, z.r, z.d)
        for t in range(1, TP):
            o = (pos + t) % TP
            send(psend.at[j, o], precv.at[j, pos], peer(t), n)
        precv[j, pos] = psend[j, pos]

    def scatter_end(j):
        n = n_rs[j]
        arrive(precv.at[j, pl.ds(0, TP - 1)], n)
        sent(precv.at[j, pl.ds(0, TP - 1)], n)
        out = precv[j, 0].astype(F32)
        for t in range(1, TP):
            out = out + precv[j, t].astype(F32)
        return out

    def vec(l, m):
        return nrm[6 * l + m][None, :]

    gather_start(gza.at[L - 1], cot.astype(BF), n_gz[L - 1])

    landed(nrm_in, nrm, 0)
    arrive(media.at[pl.ds(0, z.ny)], n_ma)
    for t in range(1, z.ny):
        yy = (y + t) % z.ny
        send(media.at[yy * 2 + c], media.at[yy * 2 + c], sib, n_mb)
    arrive(media.at[pl.ds(0, z.ny)], n_mb)

    def norm_piece(j, _):
        xhat, rstd = centre(media[j].astype(F32))
        rows = pl.ds(pl.multiple_of(j * z.pr, 8), z.pr)
        for l in range(L):
            mn[l, rows] = (xhat * vec(l, 0) + vec(l, 1)).astype(BF)
        return 0

    lax.fori_loop(0, z.ns, norm_piece, 0)

    lane_head = lax.broadcasted_iota(jnp.int32, (1, z.half), 1) // HEAD

    def stack_heads(v):
        return jnp.concatenate([jnp.where(lane_head == h, v, jnp.zeros_like(v)) for h in range(z.heads)], axis=0)

    def fold_heads(v):
        out = None
        fold[...] = v
        for h in range(z.heads):
            part = jnp.where(lane_head == h, fold[h * z.latn:(h + 1) * z.latn], 0.0)
            out = part if out is None else out + part
        return out

    key_pos = lax.broadcasted_iota(jnp.int32, (1, z.keys), 1)
    live = (key_pos < counts[y]) | (key_pos >= z.pm)

    def media_kv(l):
        kv[l, :z.pm] = dot(mn[l, :z.pm], wqkv[l, :, z.half:]).astype(BF)

    def attention(l):
        xhat, _ = centre(xs[l])
        at = pl.ds(pl.multiple_of(z.pm + c * z.r, 16), z.r)
        swap(mn.at[l, at], (xhat * vec(l, 2) + vec(l, 3)).astype(BF), n_ln[l])
        rows = mn[l, z.pm:]
        qkv = dot(rows, wqkv[l]).astype(BF)
        kv[l, z.pm:] = qkv[:, z.half:]
        q = stack_heads(qkv[:, :z.half])
        q4[l] = q
        scores = dot(q, kv[l, :, :z.half], 1, 1) * 0.125
        scores = jnp.where(live, scores, -1000000000.0)
        e = jnp.exp(scores - jnp.max(scores, axis=-1, keepdims=True))
        rt = jnp.sum(e, axis=-1, keepdims=True)
        pexp[l] = e
        rtot[l] = rt
        mixed = dot(e.astype(BF), kv[l, :, z.half:]) / rt
        own = fold_heads(mixed)
        att4[l] = own
        pair_swap(atta.at[l], own.astype(BF), n_at[l])
        mine = pl.ds(pl.multiple_of(c * z.r, 8), z.r)
        out = dot(jnp.concatenate([atta[l, 0, mine], atta[l, 1, mine]], axis=1), wo[l])
        after = xs[l] + out
        aft[l] = after
        xhat, _ = centre(after)
        gather_start(ffa.at[l], (xhat * vec(l, 4) + vec(l, 5)).astype(BF), n_ff[l])

    def hidden(l):
        gather_end(ffa.at[l], n_ff[l])
        h = dot(ffa[l].reshape(z.rows, z.d), wup[l])
        hp[l] = h
        act[l] = (h * (0.5 * (1.0 + lax.erf(h * 0.7071067811865476)))).astype(BF)

    def down(l):
        scatter_sum(dot(act[l], wdn[l]), l)

    def ff_back(l):
        gather_end(gza.at[l], n_gz[l])
        g = dot(gza[l].reshape(z.rows, z.d), wdn[l], 1, 1)
        h = hp[l]
        slope = 0.5 * (1.0 + lax.erf(h * 0.7071067811865476)) + h * 0.3989422804014327 * jnp.exp(-0.5 * h * h)
        gpre[l] = (g * slope).astype(BF)
        scatter_sum(dot(gpre[l], wup[l], 1, 1), L + l)

    def ff_grads(l):
        gdn[l] = dot(act[l], gza[l].reshape(z.rows, z.d), 0, 0).astype(BF)
        gup[l] = dot(ffa[l].reshape(z.rows, z.d), gpre[l], 0, 0).astype(BF)

    def attn_back(l, gx):
        gff = scatter_end(L + l)
        xhat, rstd = centre(aft[l])
        gn[6 * l + 4] = jnp.sum(gff * xhat, axis=0)
        gn[6 * l + 5] = jnp.sum(gff, axis=0)
        gafter = gx + pull(xhat, rstd, gff, vec(l, 4))
        pair_swap(gya.at[l], gafter.astype(BF), n_gy[l])
        gy = gya[l].reshape(z.latn, z.d)
        wo_own = wo[l, pl.ds(pl.multiple_of(c * z.half, 128), z.half)]
        gatt = dot(gy, wo_own, 1, 1).astype(BF)
        g4 = stack_heads(gatt.astype(F32))
        a4 = stack_heads(att4[l])
        delta = jnp.sum(g4 * a4, axis=-1, keepdims=True)
        rt = rtot[l]
        e = pexp[l]
        gp = dot(g4.astype(BF), kv[l, :, z.half:], 1, 1)
        gs = (e / rt * (gp - delta)).astype(BF)
        gq = (fold_heads(dot(gs, kv[l, :, :z.half])) * 0.125).astype(BF)
        gk = (dot(gs, q4[l], 0, 0) * 0.125).astype(BF)
        gv = dot(e.astype(BF), (g4 / rt).astype(BF), 0, 0).astype(BF)
        glat = jnp.concatenate([gq, gk[z.pm:], gv[z.pm:]], axis=1)
        part = dot(glat, wqkv[l], 1, 1)
        gl[l] = part.reshape(2, z.r, z.d)
        send(gl.at[l, 1 - c], grecv.at[l], sib, n_gl[l])
        gkvm[l, :, :z.half] = gk
        gkvm[l, :, z.half:] = gv
        arrive(grecv.at[l], n_gl[l])
        sent(grecv.at[l], n_gl[l])
        gln = gl[l, c] + grecv[l]
        xhat, rstd = centre(xs[l])
        gn[6 * l + 2] = jnp.sum(gln * xhat, axis=0)
        gn[6 * l + 3] = jnp.sum(gln, axis=0)
        return gafter + pull(xhat, rstd, gln, vec(l, 2)), gq

    def attn_grads(l, gq):
        gqkv[l, :, :z.half] = dot(mn[l, z.pm:], gq, 0, 0).astype(BF)
        gqkv[l, :, z.half:] = dot(mn[l], gkvm[l], 0, 0).astype(BF)
        att = jnp.concatenate([atta[l, 0], atta[l, 1]], axis=1)
        cols = pl.ds(pl.multiple_of(c * (z.d // 2), 128), z.d // 2)
        gyc = jnp.concatenate([gya[l, 0, :, cols], gya[l, 1, :, cols]], axis=0)
        gout[l] = dot(att, gyc, 0, 0).astype(BF)

    def media_back(l):
        cm[...] = dot(gkvm[l, :z.pm], wqkv[l, :, z.half:], 1, 1)

        def piece(j, sums):
            rows = pl.ds(pl.multiple_of(j * z.pr, 8), z.pr)
            xhat, rstd = centre(media[j].astype(F32))
            cotm = cm[rows]
            add = cotm * vec(l, 0)
            macc[rows] = add if l == L - 1 else macc[rows] + add
            return sums[0] + col_sum(cotm * xhat), sums[1] + col_sum(cotm)

        zero = jnp.zeros((1, z.d), F32)
        a, b = lax.fori_loop(0, z.ns, piece, (zero, zero))
        gn[6 * l + 0] = a[0]
        gn[6 * l + 1] = b[0]

    landed(*loads[1], 1)
    media_kv(0)
    landed(*loads[2], 2)
    landed(*loads[3], 3)
    landed(*loads[4], 4)
    for l in range(L):
        attention(l)
        if l == 0:
            for n in range(5, 9):
                landed(*loads[n], n)
            media_kv(1)
        hidden(l)
        if l < L - 1:
            down(l)
            xs[l + 1] = aft[l] + scatter_end(l)
    gx = cot
    for l in reversed(range(L)):
        if l < L - 1:
            gather_start(gza.at[l], gx.astype(BF), n_gz[l])
        ff_back(l)
        if l == L - 1:
            down(l)
        ff_grads(l)
        gx, gq = attn_back(l, gx)
        attn_grads(l, gq)
        media_back(l)
        if l == L - 1:
            xout[...] = (aft[l] + scatter_end(l)).astype(z.lt).reshape(z.ny, z.lr, z.d)
    gxo[...] = gx.reshape(z.ny, z.lr, z.d)

    def give_back(src, out, n):
        for j in range(z.ny):
            to = c * z.ny + j

            @pl.when(to != s)
            def _():
                send(src.at[j], out.at[y], (i, to), n)

            @pl.when(to == s)
            def _():
                pltpu.make_async_copy(src.at[j], out.at[y], rs.at[n]).start()

    give_back(xout, lat_out, n_lo)
    give_back(gxo, glat_out, n_go)
    h = z.pm // 2
    other = pl.ds(pl.multiple_of((1 - c) * h, 8), h)
    mine = pl.ds(pl.multiple_of(c * h, 8), h)
    msend[...] = macc[other].astype(z.mt)
    send(msend, mrecv, sib, n_md)
    arrive(mrecv, n_md)
    sent(mrecv, n_md)
    xhat, rstd = centre(media[pl.ds(c * z.ny, z.ny)].astype(F32).reshape(h, z.d))
    gm = pull(xhat, rstd, macc[mine] + mrecv[...].astype(F32), jnp.ones((1, z.d), F32))
    msend2 = mn.at[0, pl.ds(0, h)]
    if z.mt == BF:
        for j in range(z.ny):
            mn[0, pl.ds(j * z.pr, z.pr)] = gm[j * z.pr:(j + 1) * z.pr].astype(BF)
        srcs = [mn.at[0, pl.ds(j * z.pr, z.pr)] for j in range(z.ny)]
    else:
        macc[:h] = gm
        srcs = [macc.at[pl.ds(j * z.pr, z.pr)] for j in range(z.ny)]
    for j in range(z.ny):
        to = c * z.ny + j

        @pl.when(to != s)
        def _():
            send(srcs[j], gmedia_out.at[y], (i, to), n_mo)

        @pl.when(to == s)
        def _():
            pltpu.make_async_copy(srcs[j], gmedia_out.at[y], rs.at[n_mo]).start()

    gn_out[...] = gn[...]
    arrive(lat_out, n_lo)
    arrive(glat_out, n_go)
    arrive(gmedia_out, n_mo)
    for yy in range(z.ny):
        @pl.when(yy * 2 + s // z.ny != s)
        def _():
            pltpu.make_async_copy(lc.at[0], lc.at[0], ss.at[n_lc]).wait()
    for j in range(z.ny):
        @pl.when(c * z.ny + j != s)
        def _():
            pltpu.make_async_copy(xout.at[0], xout.at[0], ss.at[n_lo]).wait()
            pltpu.make_async_copy(gxo.at[0], gxo.at[0], ss.at[n_go]).wait()
            pltpu.make_async_copy(srcs[0], srcs[0], ss.at[n_mo]).wait()
    if z.ny > 1:
        part = media.at[pl.ds(0, z.ny - 1)]
        pltpu.make_async_copy(part, part, ss.at[n_ma]).wait()
    part = media.at[pl.ds(0, z.ny)]
    pltpu.make_async_copy(part, part, ss.at[n_mb]).wait()
    for ref, n in waits:
        pltpu.make_async_copy(ref, ref, ss.at[n]).wait()


NSEM = 32


def call(z, *args):
    L, D = z.layers, z.d
    V = lambda *shape_dtype: pltpu.VMEM(shape_dtype[:-1], shape_dtype[-1])
    out = lambda *shape_dtype: jax.ShapeDtypeStruct(shape_dtype[:-1], shape_dtype[-1])
    outs = [
        (out(z.ny, z.lr, D, z.lt), pl.ANY),
        (out(z.ny, z.pr, D, z.mt), pl.ANY),
        (out(z.ny, z.lr, D, F32), pl.ANY),
        (out(L, D, 3 * z.half, BF), pltpu.VMEM),
        (out(L, z.inner, D // 2, BF), pltpu.VMEM),
        (out(L, D, z.fs, BF), pltpu.VMEM),
        (out(L, z.fs, D, BF), pltpu.VMEM),
        (out(16, D, F32), pltpu.VMEM),
    ]
    R, T = z.r, TP
    scratch = [
        V(z.ns, z.pr, D, z.mt), V(z.ny, 2, z.lr, D, z.lt), V(L, z.keys, D, BF), V(L, z.keys, 2 * z.half, BF),
        V(L, D, 3 * z.half, BF), V(L, z.inner, D, BF), V(L, D, z.fs, BF), V(L, z.fs, D, BF), V(16, D, F32),
        V(L, z.heads * z.latn, z.half, BF), V(L, z.heads * z.latn, z.keys, F32),
        V(L, z.heads * z.latn, 1, F32), V(L, z.latn, z.half, F32), V(L, 2, z.latn, z.half, BF), V(L, R, D, F32),
        V(L, T, R, D, BF), V(L, z.rows, z.fs, F32), V(L, z.rows, z.fs, BF), V(L, R, D, F32), V(L, T, R, D, BF),
        V(2 * L, T, R, D, BF), V(2 * L, T, R, D, BF), V(L, z.rows, z.fs, BF), V(L, 2, R, D, BF), V(L, 2, R, D, F32),
        V(L, R, D, F32), V(L, z.keys, 2 * z.half, BF), V(z.pm, D, F32), V(z.pm // 2, D, z.mt), V(z.pm // 2, D, z.mt),
        V(16, D, F32), V(z.ny, z.lr, D, z.lt), V(z.ny, z.lr, D, F32), V(z.pm, D, F32), V(z.heads * z.latn, z.half, F32),
        pltpu.SemaphoreType.DMA((NSEM,)), pltpu.SemaphoreType.DMA((NSEM,)), pltpu.SemaphoreType.DMA((16,)),
    ]
    ins = [pl.ANY, pl.ANY, pltpu.SMEM] + [pl.ANY] * 5
    return pl.pallas_call(
        functools.partial(kernel, z),
        out_shape=[o for o, _ in outs],
        in_specs=[pl.BlockSpec(memory_space=m) for m in ins],
        out_specs=[pl.BlockSpec(memory_space=m) for _, m in outs],
        scratch_shapes=scratch,
        compiler_params=pltpu.CompilerParams(collective_id=0, has_side_effects=True, vmem_limit_bytes=60 * 2**20),
    )(*args)


BOTH = ("img", "seq")


def body(mesh, media, latents, counts, wq, wkv, wout, wup, wdown, norms, cotangent):
    z = Sizes(mesh, media, latents, wq, wkv, wout, wup, wdown)
    L, D = z.layers, z.d
    i, s = lax.axis_index("img"), lax.axis_index("seq")
    y, c = s // 2, s % 2
    k = i * z.ny + y
    pos = k % TP

    def pick(a, axis, index):
        return lax.dynamic_index_in_dim(a, index, axis, keepdims=False)

    gather = lambda a, axis: lax.all_gather(a, BOTH, axis=axis, tiled=True)
    nrm = gather(norms, 2).astype(F32).reshape(6 * L, D)
    nrm = jnp.pad(nrm, ((0, 16 - 6 * L), (0, 0)))
    fq = pick(gather(wq, 1).reshape(L, D, 2, z.half), 2, c)
    fkv = pick(gather(wkv, 1).reshape(L, D, 2, 2, z.half), 3, c).reshape(L, D, 2 * z.half)
    wqkv = jnp.concatenate([fq, fkv], axis=2)
    wo = gather(wout, 1)
    fup = pick(gather(wup, 1).reshape(L, D, z.dp, TP, z.fc), 3, pos).reshape(L, D, z.fs)
    fdn = pick(gather(wdown, 1).reshape(L, z.dp, TP, z.fc, D), 2, pos).reshape(L, z.fs, D)
    latcot = jnp.stack([latents, cotangent], axis=1).astype(z.lt)
    lat, gm, gla, gqkv, gout, gup, gdn, gn = call(z, media.astype(z.mt), latcot, counts, nrm, wqkv, wo, fup, fdn)

    def spread(g, shape, axis, index):
        full = jnp.zeros(shape, F32)
        return lax.dynamic_update_index_in_dim(full, g.astype(F32), index, axis)

    scat = lambda g: lax.psum_scatter(g, BOTH, scatter_dimension=1, tiled=True)
    gq = scat(spread(gqkv[:, :, : z.half], (L, D, 2, z.half), 2, c).reshape(L, D, z.inner))
    gkv = spread(gqkv[:, :, z.half :].reshape(L, D, 2, z.half), (L, D, 2, 2, z.half), 3, c)
    gkv = scat(gkv.reshape(L, D, 2 * z.inner))
    go = scat(spread(gout, (L, z.inner, 2, D // 2), 2, c).reshape(L, z.inner, D))
    gu = spread(gup.reshape(L, D, z.dp, z.fc), (L, D, z.dp, TP, z.fc), 3, pos)
    gu = scat(gu.reshape(L, D, z.ff))
    gd = spread(gdn.reshape(L, z.dp, z.fc, D), (L, z.dp, TP, z.fc, D), 2, pos)
    gd = scat(gd.reshape(L, z.ff, D))
    gnr = lax.psum_scatter(gn, BOTH, scatter_dimension=1, tiled=True)[: 6 * L].reshape(L, 6, -1)
    return lat.astype(BF), gm.astype(F32), gla, gq, gkv, go, gu, gd, gnr


def solution(mesh):
    rows = P("img", "seq", None)
    weight = P(None, BOTH, None)
    return jax.shard_map(
        functools.partial(body, mesh),
        mesh=mesh,
        in_specs=(rows, rows, P("img"), weight, weight, weight, weight, weight, P(None, None, BOTH), rows),
        out_specs=(rows, rows, rows, weight, weight, weight, weight, weight, P(None, None, BOTH)),
        check_vma=False,
    )
```

time: 2700 us -> 1850 us (0.69)
  waiting for transfers between devices: 2310 us -> 1200 us
  local copies, waits for them, and re-layouts: 76.4 us -> 443 us
  matrix products: 135 us -> 0 us
  Pallas kernels: 0 us -> 110 us
  blocking collectives: 123 us -> 37.8 us
    reduce_scatter x12 -> x5, waiting for transfers between devices: 1600 us -> 894 us  [body(): scat = lambda g: lax.psum_scatter(g, BOTH, scatter_dimension=1, tiled=True)]
    dynamic_update_slice x0 -> x4, local copies, waits for them, and re-layouts: none -> 256 us  [spread(): return lax.dynamic_update_index_in_dim(full, g.astype(F32), index, axis)]
    all_gather x10 -> x5, waiting for transfers between devices: 501 us -> 304 us  [body(): gather = lambda a, axis: lax.all_gather(a, BOTH, axis=axis, tiled=True)]
    unnamed x28 -> x12, waiting for transfers between devices: 177 us -> 3.21 us
    dot_general x48 -> x0, matrix products: 135 us -> none  [the longest x12 50.5 us: weight_grad(): jnp.einsum('ird,ire->de', left, grads, preferred_element_type=jnp.float32)]
    pallas_call x0 -> x1, Pallas kernels: none -> 110 us  [call(): pl.pallas_call(functools.partial(kernel, z), out_shape=[o for o, _ in out...]
    reshape x14 -> x10, local copies, waits for them, and re-layouts: 12.4 us -> 76.8 us  [the longest x1 35.9 us: body(): gu = scat(gu.reshape(L, D, z.ff))]
    all_gather x6 -> x1, blocking collectives: 99.7 us -> 37.8 us  [body(): gather = lambda a, axis: lax.all_gather(a, BOTH, axis=axis, tiled=True)]
  transfers between devices with their start and end apart: 26 -> 11, of which waited for: 24 -> 9; matrix products, arithmetic and copies ran while one was open for 6% -> 25% of each run, Pallas kernels for 0% -> 0%
where the time goes in v1:
time: 1850 us; the launch traced here: 1820 us
  waiting for transfers between devices  1200 us (65%)
  local copies, waits for them, and re-layouts  443 us (24%)
  Pallas kernels  110 us (6%)
  blocking collectives  37.8 us (2%)
    reduce_scatter x5, waiting for transfers between devices, body(): scat = lambda g: lax.psum_scatter(g, BOTH, scatter_dimension=1, tiled=True)  894 us
    all_gather x5, waiting for transfers between devices, body(): gather = lambda a, axis: lax.all_gather(a, BOTH, axis=axis, tiled=True)  304 us
    dynamic_update_slice x4, local copies, waits for them, and re-layouts, spread(): return lax.dynamic_update_index_in_dim(full, g.astype(F32), index, axis)  256 us
    pallas_call x1, Pallas kernels, call(): pl.pallas_call(functools.partial(kernel, z), out_shape=[o for o, _ in out...  110 us
    all_gather x1, blocking collectives, body(): gather = lambda a, axis: lax.all_gather(a, BOTH, axis=axis, tiled=True)  37.8 us
    dynamic_slice x4, local copies, waits for them, and re-layouts, pick(): return lax.dynamic_index_in_dim(a, index, axis, keepdims=False)  37.5 us
  transfers between devices with their start and end apart: 11, of which 9 were waited for; matrix products, arithmetic and copies ran while one was open for 25% of the time, Pallas kernels for 0%

profile of v1, /device:TPU:9, one launch (start us, length us, event | category | flops | bytes accessed | tf_op | source)
XLA Modules:
  0.0 1820.8 jit_solution(11110128824178704978)
XLA Ops:
  11.4 37.8 %all_gather.18 = bf16[2,6,1024]{1,0,2:T(2,128)(2,1)S(1)} all-gather(bf16[2,6,32]{1,0,2:T(2,128)(2,1)S(1)} %copy.41), channel_id=1, replica_groups=mesh['img'=8,'seq'=4] {'img','seq'}, dimensions={2}, use_global_device_ids=true | all-gather | bytes 25344 | tf_op jit(solution)/shard_map/all_gather | solution.py:485
  51.9 16.6 all-gather.6.cloned.1.call-done
  73.4 59.8 %all-gather.8.cloned.1.call-done = bf16[2,1024,1024]{2,1,0:T(8,128)(2,1)} async-done(((bf16[2,32,1024]{2,1,0:T(8,128)(2,1)}), bf16[2,1024,1024]{2,1,0:T(8,128)(2,1)}) %all-gather.8.cloned.1.call-update) | async-done | bytes 4194320 | tf_op jit(solution)/shard_map/all_gather | solution.py:485
  133.2 7.8 reshape.105
  141.1 16.9 dynamic-slice_reduce_fusion.1
  163.0 85.4 %all-gather.12.cloned.1.call-done = bf16[2,1024,4096]{2,1,0:T(8,128)(2,1)} async-done(((bf16[2,32,4096]{2,1,0:T(8,128)(2,1)}), bf16[2,1024,4096]{2,1,0:T(8,128)(2,1)}) %all-gather.12.cloned.1.call-update) | async-done | bytes 16777232 | tf_op jit(solution)/shard_map/all_gather | solution.py:485
  248.4 10.3 copy.60
  258.7 15.3 dynamic-slice_reduce_fusion
  276.7 87.5 %all-gather.14.cloned.1.call-done = bf16[2,4096,1024]{2,1,0:T(8,128)(2,1)} async-done(((bf16[2,128,1024]{2,1,0:T(8,128)(2,1)}), bf16[2,4096,1024]{2,1,0:T(8,128)(2,1)}) %all-gather.14.cloned.1.call-update) | async-done | bytes 16777232 | tf_op jit(solution)/shard_map/all_gather | solution.py:485
  367.3 54.6 %all-gather.10.cloned.1.call-done.wo_in = bf16[2,512,1024]{2,1,0:T(8,128)(2,1)} async-done(((bf16[2,16,1024]{2,1,0:T(8,128)(2,1)}), bf16[2,512,1024]{2,1,0:T(8,128)(2,1)}) %all-gather.10.cloned.1.call-update) | async-done | bytes 2097168 | tf_op jit(solution)/shard_map/all_gather | solution.py:485
  421.9 110.4 %shard_map.169 = (bf16[2,16,1024]{2,1,0:T(8,128)(2,1)}, bf16[2,144,1024]{2,1,0:T(8,128)(2,1)}, f32[2,16,1024]{2,1,0:T(8,128)}, bf16[2,1024,768]{2,1,0:T(8,128)(2...) custom-call(bf16[2,144,1024]{2,1,0:T(8,128)(2,1)} %media_in.1, ...), custom_call_target="tpu_custom_call" | custom-call | tf_op jit(solution)/shard_map/pallas_call | solution.py:461
  541.0 38.0 %dynamic_update_slice.22 = f32[2,512,2,512]{3,2,1,0:T(2,128)} dynamic-update-slice(f32[2,512,2,512]{3,2,1,0:T(2,128)} %broadcast_in_dim.39, f32[2,512,1,512]{3,2,1,0:T(1,128)S(1)} %copy.49, s32[]{:T(128)} %constant.79.clone.1, s32[]{:T(128)} %constant.79.clone.1, s32[]{:T(128)S(6)} %select_n.38, s32[]{:T(128)} %constant.79.clone.1) | dynamic-update-slice | bytes 4194308 | tf_op jit(solution)/shard_map/jit(dynamic_update_index_in_dim)/dynamic_update_slice | solution.py:499
  592.5 42.6 %dynamic_update_slice.20 = f32[2,1024,2,256]{3,2,1,0:T(2,128)} dynamic-update-slice(f32[2,1024,2,256]{3,2,1,0:T(2,128)} %broadcast_in_dim.35, f32[2,1024,1,256]{3,2,1,0:T(1,128)S(1)} %copy.47, s32[]{:T(128)} %constant.79.clone.1, s32[]{:T(128)} %constant.79.clone.1, s32[]{:T(128)S(6)} %select_n.38, s32[]{:T(128)} %constant.79.clone.1) | dynamic-update-slice | bytes 4194308 | tf_op jit(solution)/shard_map/jit(dynamic_update_index_in_dim)/dynamic_update_slice | solution.py:499
  646.0 7.7 reshape.124
  659.0 82.8 %dynamic_update_slice.21 = f32[2,1024,2,2,256]{4,3,2,1,0:T(2,128)} dynamic-update-slice(f32[2,1024,2,2,256]{4,3,2,1,0:T(2,128)} %broadcast_in_dim.38, f32[2,1024,2,1,256]{4,3,2,1,0:T(1,128)} %reshape.124, s32[]{:T(128)} %constant.79.clone.1, s32[]{:T(128)} %constant.79.clone.1, s32[]{:T(128)} %constant.79.clone.1, s32[]{:T(128)S(6)} %select_n.38, s32[]{:T(128)} %constant.79.clone.1) | dynamic-update-slice | bytes 8388612 | tf_op jit(solution)/shard_map/jit(dynamic_update_index_in_dim)/dynamic_update_slice | solution.py:499
  741.8 11.6 reshape.112
  753.5 11.4 broadcast_in_dim.43
  769.0 6.7 reshape.125
  775.7 11.3 broadcast_in_dim.42
  787.0 92.2 %dynamic_update_slice.23 = f32[2,1024,2,8,256]{4,3,2,1,0:T(8,128)} dynamic-update-slice(f32[2,1024,2,8,256]{4,3,2,1,0:T(8,128)} %broadcast_in_dim.42, f32[2,1024,2,1,256]{4,3,2,1,0:T(1,128)} %reshape.125, s32[]{:T(128)} %constant.79.clone.1, s32[]{:T(128)} %constant.79.clone.1, s32[]{:T(128)} %constant.79.clone.1, s32[]{:T(128)S(6)} %select_n.41, s32[]{:T(128)} %constant.79.clone.1) | dynamic-update-slice | bytes 8388612 | tf_op jit(solution)/shard_map/jit(dynamic_update_index_in_dim)/dynamic_update_slice | solution.py:499
  879.2 35.9 %reshape.114 = f32[2,1024,4096]{2,1,0:T(8,128)} reshape(f32[2,1024,2,8,256]{4,3,2,1,0:T(8,128)} %dynamic_update_slice.23) | data formatting | bytes 67108864 | tf_op jit(solution)/shard_map/reshape | solution.py:507
  923.2 149.1 %reduce-scatter.11.cloned.1.call-done = f32[2,32,1024]{2,1,0:T(8,128)} async-done(((f32[2,1024,1024]{2,1,0:T(8,128)}), f32[2,32,1024]{2,1,0:T(8,128)}) %reduce-scatter.11.cloned.1.call-update) | async-done | bytes 262160 | tf_op jit(solution)/shard_map/reduce_scatter | solution.py:501
  1072.3 379.8 %reduce-scatter.17.cloned.1.call-done = f32[2,128,1024]{2,1,0:T(8,128)} async-done(((f32[2,4096,1024]{2,1,0:T(8,128)}), f32[2,128,1024]{2,1,0:T(8,128)}) %reduce-scatter.17.cloned.1.call-update) | async-done | bytes 1048592 | tf_op jit(solution)/shard_map/reduce_scatter | solution.py:501
  1452.1 360.6 %reduce-scatter.15.cloned.1.call-done = f32[2,32,4096]{2,1,0:T(8,128)} async-done(((f32[2,1024,4096]{2,1,0:T(8,128)}), f32[2,32,4096]{2,1,0:T(8,128)}) %reduce-scatter.15.cloned.1.call-update) | async-done | bytes 1048592 | tf_op jit(solution)/shard_map/reduce_scatter | solution.py:501
  (67 shorter events, 74.2 us)
Async XLA Ops:
  7.2 61.3 %all-gather.6.cloned.1.call-start = ((), (), s32[]{:S(2)}) async-start(), calls=%async_computation.6 | async-start | bytes 2162688 | tf_op jit(solution)/shard_map/all_gather | solution.py:485
  7.9 125.3 %all-gather.8.cloned.1.call-start = ((), (), s32[]{:S(2)}) async-start(), calls=%async_computation.7 | async-start | bytes 4325376 | tf_op jit(solution)/shard_map/all_gather | solution.py:485
  8.7 239.8 %all-gather.12.cloned.1.call-start = ((), (), s32[]{:S(2)}) async-start(), calls=%async_computation.9 | async-start | bytes 17301504 | tf_op jit(solution)/shard_map/all_gather | solution.py:485
  9.4 354.8 %all-gather.14.cloned.1.call-start = ((), (), s32[]{:S(2)}) async-start(), calls=%async_computation.10 | async-start | bytes 17301504 | tf_op jit(solution)/shard_map/all_gather | solution.py:485
  10.0 412.0 %all-gather.10.cloned.1.call-start = ((), (), s32[]{:S(2)}) async-start(), calls=%async_computation.8 | async-start | bytes 2162688 | tf_op jit(solution)/shard_map/all_gather | solution.py:485
  10.6 906.8 %reduce-scatter.19.cloned.1.call-start = ((), (), s32[]{:S(2)}) async-start(), calls=%async_computation.16 | async-start | bytes 540672
  534.2 384.5 %reduce-scatter.13.cloned.1.call-start = ((), (), s32[]{:S(2)}) async-start(), calls=%async_computation.13 | async-start | bytes 4325376 | tf_op jit(solution)/shard_map/reduce_scatter | solution.py:501
  585.7 337.5 %reduce-scatter.9.cloned.1.call-start = ((), (), s32[]{:S(2)}) async-start(), calls=%async_computation.11 | async-start | bytes 4325376 | tf_op jit(solution)/shard_map/reduce_scatter | solution.py:501
  641.5 1.9 copy-start
  641.5 430.8 %reduce-scatter.11.cloned.1.call-start = ((), (), s32[]{:S(2)}) async-start(), calls=%async_computation.12 | async-start | bytes 8650752 | tf_op jit(solution)/shard_map/reduce_scatter | solution.py:501
  753.4 698.7 %reduce-scatter.17.cloned.1.call-start = ((), (), s32[]{:S(2)}) async-start(), calls=%async_computation.15 | async-start | bytes 34603008 | tf_op jit(solution)/shard_map/reduce_scatter | solution.py:501
  753.4 11.4 copy-start.2
  767.4 1.6 copy-start.1
  767.4 1045.3 %reduce-scatter.15.cloned.1.call-start = ((), (), s32[]{:S(2)}) async-start(), calls=%async_computation.14 | async-start | bytes 34603008 | tf_op jit(solution)/shard_map/reduce_scatter | solution.py:501
  915.1 1.1 copy-start.3
  915.1 897.6 %copy-start.5 = (bf16[2,16,1024]{2,1,0:T(8,128)(2,1)S(1)}, bf16[2,16,1024]{2,1,0:T(8,128)(2,1)}, u32[]{:S(2)}) copy-start(bf16[2,16,1024]{2,1,0:T(8,128)(2,1)} %get-tuple-element.61) | copy-start | bytes 196612
  915.1 898.2 %copy-start.4 = (f32[2,16,1024]{2,1,0:T(8,128)S(1)}, f32[2,16,1024]{2,1,0:T(8,128)}, u32[]{:S(2)}) copy-start(f32[2,16,1024]{2,1,0:T(8,128)} %get-tuple-element.63) | copy-start | bytes 393220
Sparse Core Ops, SparseCore 0:
  10.9 57.5 all-gather.5
  71.4 61.7 all-gather.7
  136.2 112.1 all-gather.11
  251.2 112.9 all-gather.13
  367.0 54.9 all-gather.9
  534.4 109.1 reduce-scatter.18
  646.5 136.5 reduce-scatter.12
  786.0 137.1 reduce-scatter.8
  926.2 146.0 reduce-scatter.10
  1075.1 376.9 reduce-scatter.16
  1455.1 357.5 reduce-scatter.14

commit v2 on v1

v2 whole, which is shorter than its diff:
```python
import functools
import types

import jax
import jax.numpy as jnp
from jax import lax
from jax.experimental import pallas as pl
from jax.experimental.pallas import tpu as pltpu
from jax.sharding import PartitionSpec as P

HEAD = 64
EPS = 1e-05
MESH = pl.DeviceIdType.MESH
BF = jnp.bfloat16
F32 = jnp.float32
TP = 8
BOTH = ("img", "seq")


class Sizes:
    def __init__(self, mesh, media, latents, wq, wkv, wout, wup, wdown):
        self.ni, self.ns = mesh.shape["img"], mesh.shape["seq"]
        self.ny = self.ns // 2
        self.chips = self.ni * self.ny
        self.layers = wq.shape[0]
        self.d = media.shape[2]
        self.nimg, self.pr = media.shape[0], media.shape[1]
        self.lr = latents.shape[1]
        self.inner = wq.shape[2]
        self.half = self.inner // 2
        self.ff = wup.shape[2]
        self.fs = self.ff // TP
        self.dp = self.chips // TP
        self.fc = self.ff // self.chips
        self.pm = self.pr * self.ns
        self.latn = self.lr * self.ns
        self.r = self.latn // 2
        self.keys = self.pm + self.latn
        self.heads = self.half // HEAD
        self.rows = TP * self.r
        self.mt = BF if self.pr % 16 == 0 else F32
        self.lt = BF if self.lr % 16 == 0 else F32
        self.rq, self.ro, self.rd = wq.shape[1], wout.shape[1], wdown.shape[1]
        self.lanes = self.d // self.ni
        whole_tiles = all(v % 16 == 0 for v in (self.rq, self.ro, self.rd))
        whole_tiles = whole_tiles and self.fc % 128 == 0 and self.lanes % 128 == 0
        self.fused = whole_tiles and self.ny == 2 and self.ni % 4 == 0
        self.blk = (self.ni // 2, 2, self.ny) if self.fused else (2, 1, 1)
        self.nblk = self.blk[0] * self.blk[1] * self.blk[2]
        self.qrows = self.d // self.nblk
        self.orows = self.inner // self.nblk
        self.wide = 3 * self.half + self.d // 4
        assert self.nimg == self.ny and TP % self.ny == 0


def dot(a, b, ca=1, cb=0):
    return lax.dot_general(a, b, (((ca,), (cb,)), ((), ())), preferred_element_type=F32)


def centre(v):
    c = v - jnp.mean(v, axis=-1, keepdims=True)
    rstd = lax.rsqrt(jnp.mean(c * c, axis=-1, keepdims=True) + EPS)
    return c * rstd, rstd


def pull(xhat, rstd, cot, gain):
    g = cot * gain
    m1 = jnp.mean(g, axis=-1, keepdims=True)
    m2 = jnp.mean(g * xhat, axis=-1, keepdims=True)
    return rstd * (g - m1 - xhat * m2)


def col_sum(v):
    return jnp.sum(v, axis=0, keepdims=True)


def inputs_of(z):
    any_ = pl.ANY
    names = [("media_in", any_), ("latcot_in", any_), ("counts", pltpu.SMEM), ("nrm_in", any_)]
    if z.fused:
        names += [("wq_in", any_), ("wkv_in", any_), ("wo_in", any_), ("wup_in", any_), ("wdn_in", any_)]
    else:
        names += [("wqkv_in", any_), ("wo_in", any_), ("wup_in", any_), ("wdn_in", any_)]
    return names


def outputs_of(z):
    L, D = z.layers, z.d
    outs = dict(
        lat_out=(pl.ANY, (z.ny, z.lr, D), z.lt),
        gmedia_out=(pl.ANY, (z.ny, z.pr, D), z.mt),
        glat_out=(pl.ANY, (z.ny, z.lr, D), F32),
    )
    if z.fused:
        outs.update(
            gq_out=(pltpu.VMEM, (L, z.rq, z.inner), F32),
            gkv_out=(pltpu.VMEM, (L, z.rq, 2 * z.inner), F32),
            go_out=(pltpu.VMEM, (L, z.ro, D), F32),
            gup_out=(pltpu.VMEM, (L, z.rq, z.ff), F32),
            gdn_out=(pltpu.VMEM, (L, z.rd, D), F32),
            gn_out=(pltpu.VMEM, (16, z.lanes), F32),
        )
    else:
        outs.update(
            gat_out=(pl.ANY, (L, *z.blk, z.qrows, z.wide), BF),
            gup_out=(pl.ANY, (L, z.chips if z.fused else 1, 2, D // 2 if not z.fused else z.rq, z.fs), BF),
            gdn_out=(pl.ANY, (L, 1, 2, z.fs // 2, D), BF),
            gn_out=(pltpu.VMEM, (16, D), F32),
        )
    return outs


def scratch_of(z):
    L, D, R, T = z.layers, z.d, z.r, TP
    kq = z.heads * z.latn
    cu = z.chips if z.fused else 1
    gd = z.dp if z.fused else 1
    v = dict(
        media=((z.ns, z.pr, D), z.mt),
        lc=((z.ny, 2, z.lr, D), z.lt),
        mn=((L, z.keys, D), BF),
        kv=((L, z.keys, 2 * z.half), BF),
        wqkv=((L, *z.blk, z.qrows, 3 * z.half), BF),
        wo=((L, *z.blk, 2, z.orows // 2, D), BF),
        wup=((L, cu, 2, D // (2 * cu), z.fs), BF),
        wdn=((L, gd, 2, z.fs // (2 * gd), D), BF),
        nrm=((16, D), F32),
        q4=((L, kq, z.half), BF),
        pexp=((L, kq, z.keys), F32),
        rtot=((L, kq, 1), F32),
        att4=((L, z.latn, z.half), F32),
        atta=((L, 2, z.latn, z.half), BF),
        aft=((L, R, D), F32),
        ffa=((L, T, R, D), BF),
        hp=((L, z.rows, z.fs), F32),
        act=((L, z.rows, z.fs), BF),
        xs=((L, R, D), F32),
        gza=((L, T, R, D), BF),
        psend=((2 * L, T, R, D), BF),
        precv=((2 * L, T, R, D), BF),
        gpre=((L, z.rows, z.fs), BF),
        gya=((L, 2, R, D), BF),
        gl=((L, 2, R, D), F32),
        grecv=((L, R, D), F32),
        gkvm=((L, z.keys, 2 * z.half), BF),
        macc=((z.pm, D), F32),
        msend=((z.pm // 2, D), z.mt),
        mrecv=((z.pm // 2, D), z.mt),
        gn=((16, D), F32),
        xout=((z.ny, z.lr, D), z.lt),
        gxo=((z.ny, z.lr, D), F32),
        cm=((z.pm, D), F32),
        fold=((kq, z.half), F32),
        gat=((L, *z.blk, z.qrows, z.wide), BF),
        gup=((L, cu, 2, D // (2 * cu), z.fs), BF),
        gdn=((L, gd, 2, z.fs // (2 * gd), D), BF),
    )
    if z.fused:
        za = z.blk[0]
        v.update(
            nrecv=((z.ni, z.ns, 16, z.lanes), BF),
            ra=((L, za, 2, z.qrows, z.wide), BF),
            sa=((L, za, 2, z.qrows, z.wide), BF),
            rb=((L, za, z.qrows, z.wide), BF),
            sb=((L, za, z.qrows, z.wide), BF),
            rc=((L, za, z.qrows, z.wide), BF),
            sf=((L, z.qrows, z.wide), F32),
            rf=((L, z.qrows, z.wide), F32),
            updr=((L, z.chips, z.rq, z.fs), BF),
            ups=((L, z.chips, z.rq, z.fs), BF),
            upr=((L, z.chips, z.rq, z.fs), BF),
            dndr=((L, z.dp, z.rd, D), BF),
            dns=((L, z.dp, z.rd, D), BF),
            dnr=((L, z.dp, z.rd, D), BF),
            gns=((16, D), F32),
            gnd=((16, D), F32),
            gnr=((z.chips, 16, z.lanes), F32),
        )
    out = {n: pltpu.VMEM(s, d) for n, (s, d) in v.items()}
    out.update(ss=pltpu.SemaphoreType.DMA((NSEM,)), rs=pltpu.SemaphoreType.DMA((NSEM,)), ls=pltpu.SemaphoreType.DMA((16,)))
    return out


NSEM = 80


def kernel(z, names, *refs):
    L = z.layers
    q = types.SimpleNamespace(**dict(zip(names, refs)))
    ss, rs, ls = q.ss, q.rs, q.ls
    i = lax.axis_index("img")
    s = lax.axis_index("seq")
    y, c = s // 2, s % 2
    k = i * z.ny + y
    pos, grp = k % TP, k // TP
    sib = (i, y * 2 + (1 - c))
    a, b = i // 2, i % 2

    def chip(kk, cc):
        return (kk // z.ny, (kk % z.ny) * 2 + cc)

    def peer(t):
        return chip(grp * TP + (pos + t) % TP, c)

    waits = []
    used = [0]

    def sem():
        used[0] += 1
        return used[0] - 1

    def send(src, dst, dev, n):
        pltpu.make_async_remote_copy(src, dst, ss.at[n], rs.at[n], device_id=dev, device_id_type=MESH).start()

    def keep(src, dst, n):
        pltpu.make_async_copy(src, dst, rs.at[n]).start()

    def arrive(ref, n):
        pltpu.make_async_copy(ref, ref, rs.at[n]).wait()

    def gone(ref, n):
        pltpu.make_async_copy(ref, ref, ss.at[n]).wait()

    def sent(ref, n):
        waits.append((ref, n))

    bar = pltpu.get_barrier_semaphore()
    total = z.ni * z.ns
    me = i * z.ns + s

    def greet(t, _):
        o = (me + t) % total
        pl.semaphore_signal(bar, inc=1, device_id=(o // z.ns, o % z.ns), device_id_type=MESH)
        return 0

    lax.fori_loop(1, total, greet, 0)
    pl.semaphore_wait(bar, total - 1)

    def lanes(start, size):
        return pl.ds(pl.multiple_of(start, 128), size)

    def at16(start, size):
        return pl.ds(pl.multiple_of(start, 16), size)

    H = z.half
    if z.fused:
        za = z.blk[0]
        n_w0, n_q1, n_q2, n_q3 = ([sem() for _ in range(L)] for _ in range(4))
        n_o0, n_o1, n_o2, n_o3, n_od = ([sem() for _ in range(L)] for _ in range(5))
        n_ua, n_ub, n_da, n_db = ([sem() for _ in range(L)] for _ in range(4))
        n_nrm = sem()
        xdev = (i + 1 - 2 * b, s)
        ydev = (i, (1 - y) * 2 + c)
        first = (xdev[0] * (1 - c) + i * c, s * (1 - c) + ydev[1] * c)
        second = (i * (1 - c) + xdev[0] * c, ydev[1] * (1 - c) + s * c)

        def weights_pair(l):
            rows = at16(c * z.rq, z.rq)
            block = q.wqkv.at[l, a, b, y, rows]
            for cc, dev in ((c, None), (1 - c, sib)):
                for src, off in ((q.wq_in.at[l, :, lanes(cc * H, H)], 0), (q.wkv_in.at[l, :, lanes(cc * H, H)], H),
                                 (q.wkv_in.at[l, :, lanes(z.inner + cc * H, H)], 2 * H)):
                    dst = block.at[:, pl.ds(off, H)]
                    if dev is None:
                        keep(src, dst, n_w0[l])
                    else:
                        send(src, dst, dev, n_w0[l])
            sent(q.wqkv.at[l, 0, 0, 0, pl.ds(0, z.rq)], n_w0[l])
            keep(q.wo_in.at[l], q.wo.at[l, a, b, y, c], n_o0[l])

        def weights_z(l):
            arrive(q.wqkv.at[l, a, b, y], n_w0[l])
            for t in range(1, za):
                dev = (((a + t) % za) * 2 + b, s)
                send(q.wqkv.at[l, a, b, y], q.wqkv.at[l, a, b, y], dev, n_q1[l])
            arrive(q.wo.at[l, a, b, y, c], n_o0[l])
            for t in range(1, za):
                dev = (((a + t) % za) * 2 + b, s)
                send(q.wo.at[l, a, b, y, c], q.wo.at[l, a, b, y, c], dev, n_o1[l])

        def weights_first(l):
            part = q.wqkv.at[l, pl.ds(0, za - 1), 0, 0]
            arrive(part, n_q1[l])
            sent(part, n_q1[l])
            send(q.wqkv.at[l, :, b, y], q.wqkv.at[l, :, b, y], first, n_q2[l])
            part = q.wo.at[l, pl.ds(0, za - 1), 0, 0, 0]
            arrive(part, n_o1[l])
            sent(part, n_o1[l])
            send(q.wo.at[l, :, b, y, c], q.wo.at[l, :, b, y, c], first, n_o2[l])

        def weights_second(l):
            for buf, n2, n3, tail in ((q.wqkv, n_q2[l], n_q3[l], ()), (q.wo, n_o2[l], n_o3[l], (c,))):
                part = buf.at[(l, slice(None), 0, 0) + ((0,) if tail else ())]
                arrive(part, n2)
                sent(part, n2)
                mid = (slice(None),) * 2 if tail else ()

                @pl.when(c == 0)
                def _():
                    ref = buf.at[(l, slice(None), slice(None), y) + ((0,) if tail else ())]
                    send(ref, ref, second, n3)

                @pl.when(c == 1)
                def _():
                    ref = buf.at[(l, slice(None), b) + ((slice(None), 1) if tail else ())]
                    send(ref, ref, second, n3)

        def weights_qkv_end(l):
            part = q.wqkv.at[l, :, 0]
            arrive(part, n_q3[l])
            sent(part, n_q3[l])

        def weights_out_share(l):
            part = q.wo.at[l, :, 0, :, 0]
            arrive(part, n_o3[l])
            sent(part, n_o3[l])
            ref = q.wo.at[l, :, :, :, c]
            send(ref, ref, sib, n_od[l])

        def weights_out_end(l):
            ref = q.wo.at[l, :, :, :, 0]
            arrive(ref, n_od[l])
            sent(ref, n_od[l])

        def weights_ff(l):
            def one(t, _):
                kk = (k + t) % z.chips
                dev = chip(kk, c)
                for g in range(z.dp):
                    src = q.wup_in.at[l, :, lanes((g * TP + kk % TP) * z.fc, z.fc)]
                    send(src, q.wup.at[l, k, c, :, pl.ds(g * z.fc, z.fc)], dev, n_ua[l])
                return 0

            for g in range(1, z.dp):
                dev = chip(((grp + g) % z.dp) * TP + pos, c)
                send(q.wdn_in.at[l], q.wdn.at[l, grp, c], dev, n_da[l])
            keep(q.wdn_in.at[l], q.wdn.at[l, grp, c], n_da[l])
            lax.fori_loop(1, z.chips, one, 0)
            for g in range(z.dp):
                src = q.wup_in.at[l, :, lanes((g * TP + pos) * z.fc, z.fc)]
                keep(src, q.wup.at[l, k, c, :, pl.ds(g * z.fc, z.fc)], n_ua[l])
            sent(q.wup.at[l, pl.ds(0, z.chips - 1), 0], n_ua[l])
            sent(q.wdn.at[l, pl.ds(0, z.dp - 1), 0], n_da[l])

        def weights_ff_share(l):
            arrive(q.wup.at[l, :, 0], n_ua[l])
            send(q.wup.at[l, :, c], q.wup.at[l, :, c], sib, n_ub[l])
            arrive(q.wdn.at[l, :, 0], n_da[l])
            send(q.wdn.at[l, :, c], q.wdn.at[l, :, c], sib, n_db[l])

        def weights_ff_end(l):
            arrive(q.wup.at[l, :, 0], n_ub[l])
            sent(q.wup.at[l, :, 0], n_ub[l])
            arrive(q.wdn.at[l, :, 0], n_db[l])
            sent(q.wdn.at[l, :, 0], n_db[l])

        def norms_start():
            def one(t, _):
                o = (me + t) % total
                send(q.nrm_in, q.nrecv.at[i, s], (o // z.ns, o % z.ns), n_nrm)
                return 0

            lax.fori_loop(1, total, one, 0)
            keep(q.nrm_in, q.nrecv.at[i, s], n_nrm)

        def norms_end():
            arrive(q.nrecv, n_nrm)
            for ii in range(z.ni):
                v = q.nrecv[ii, 0].astype(F32)
                for j in range(1, z.ns):
                    v = v + q.nrecv[ii, j].astype(F32)
                q.nrm[:, ii * z.lanes:(ii + 1) * z.lanes] = v
    else:
        loads = [(q.nrm_in, q.nrm)]
        for l in range(L):
            loads += [(getattr(q, n + "_in").at[l], getattr(q, n).at[l]) for n in ("wqkv", "wo", "wup", "wdn")]

        def norms_start():
            for n, (src, dst) in enumerate(loads):
                pltpu.make_async_copy(src, dst, ls.at[n]).start()

        def load_end(n):
            pltpu.make_async_copy(*loads[n], ls.at[n]).wait()

        def norms_end():
            load_end(0)

        def nothing(l):
            pass

        weights_pair = weights_z = weights_first = weights_second = nothing
        weights_out_share = weights_ff = weights_ff_share = nothing

        def weights_qkv_end(l):
            load_end(1 + 4 * l)

        def weights_out_end(l):
            load_end(2 + 4 * l)

        def weights_ff_end(l):
            load_end(3 + 4 * l)
            load_end(4 + 4 * l)

    def w_qkv(l):
        return q.wqkv[l].reshape(z.d, 3 * H)

    def w_kv(l):
        return q.wqkv[l, :, :, :, :, H:].reshape(z.d, 2 * H)

    def w_up(l):
        return q.wup[l].reshape(z.d, z.fs)

    def w_dn(l):
        return q.wdn[l].reshape(z.fs, z.d)

    n_lc, n_ma, n_mb = sem(), sem(), sem()
    n_ff, n_gz, n_ln, n_at, n_gy, n_gl = ([sem() for _ in range(L)] for _ in range(6))
    n_rs = [sem() for _ in range(2 * L)]
    n_md, n_lo, n_go, n_mo = sem(), sem(), sem(), sem()
    own_slot = s % z.ny

    def rows_start():
        for t in range(1, z.ny):
            yy = (y + t) % z.ny
            send(q.media_in.at[yy], q.media.at[s], (i, yy * 2 + c), n_ma)
        keep(q.media_in.at[y], q.media.at[s], n_ma)
        send(q.media_in.at[y], q.media.at[s], sib, n_mb)
        for yy in range(z.ny):
            to = yy * 2 + s // z.ny

            @pl.when(to != s)
            def _():
                send(q.latcot_in.at[yy], q.lc.at[own_slot], (i, to), n_lc)

            @pl.when(to == s)
            def _():
                keep(q.latcot_in.at[yy], q.lc.at[own_slot], n_lc)

    def media_share():
        arrive(q.media.at[pl.ds(0, z.ny)], n_ma)
        for t in range(1, z.ny):
            yy = (y + t) % z.ny
            send(q.media.at[yy * 2 + c], q.media.at[yy * 2 + c], sib, n_mb)

    def rows_sent():
        for yy in range(z.ny):
            @pl.when(yy * 2 + s // z.ny != s)
            def _():
                gone(q.lc.at[0], n_lc)
        if z.ny > 1:
            gone(q.media.at[pl.ds(0, z.ny - 1)], n_ma)
        gone(q.media.at[pl.ds(0, z.ny)], n_mb)

    def gather_start(buf, value, n):
        buf[pos] = value
        for t in range(1, TP):
            send(buf.at[pos], buf.at[pos], peer(t), n)

    def gather_end(buf, n):
        arrive(buf.at[pl.ds(0, TP - 1)], n)
        sent(buf.at[pl.ds(0, TP - 1)], n)

    def swap(ref, value, n):
        ref[...] = value
        send(ref, ref, sib, n)
        arrive(ref, n)
        sent(ref, n)

    def scatter_sum(part, j):
        q.psend[j] = part.astype(BF).reshape(TP, z.r, z.d)
        for t in range(1, TP):
            o = (pos + t) % TP
            send(q.psend.at[j, o], q.precv.at[j, pos], peer(t), n_rs[j])
        q.precv[j, pos] = q.psend[j, pos]

    def scatter_end(j):
        arrive(q.precv.at[j, pl.ds(0, TP - 1)], n_rs[j])
        sent(q.precv.at[j, pl.ds(0, TP - 1)], n_rs[j])
        out = q.precv[j, 0].astype(F32)
        for t in range(1, TP):
            out = out + q.precv[j, t].astype(F32)
        return out

    def vec(l, m):
        return q.nrm[6 * l + m][None, :]

    lane_head = lax.broadcasted_iota(jnp.int32, (1, H), 1) // HEAD

    def stack_heads(v):
        return jnp.concatenate([jnp.where(lane_head == h, v, jnp.zeros_like(v)) for h in range(z.heads)], axis=0)

    def fold_heads(v):
        out = None
        q.fold[...] = v
        for h in range(z.heads):
            part = jnp.where(lane_head == h, q.fold[h * z.latn:(h + 1) * z.latn], 0.0)
            out = part if out is None else out + part
        return out

    key_pos = lax.broadcasted_iota(jnp.int32, (1, z.keys), 1)
    live = (key_pos < q.counts[y]) | (key_pos >= z.pm)

    def norm_piece(j, _):
        xhat, _ = centre(q.media[j].astype(F32))
        rows = pl.ds(pl.multiple_of(j * z.pr, 8), z.pr)
        for l in range(L):
            q.mn[l, rows] = (xhat * vec(l, 0) + vec(l, 1)).astype(BF)
        return 0

    def media_kv(l):
        q.kv[l, :z.pm] = dot(q.mn[l, :z.pm], w_kv(l)).astype(BF)

    def attention(l):
        xhat, _ = centre(q.xs[l])
        swap(q.mn.at[l, at16(z.pm + c * z.r, z.r)], (xhat * vec(l, 2) + vec(l, 3)).astype(BF), n_ln[l])
        qkv = dot(q.mn[l, z.pm:], w_qkv(l)).astype(BF)
        q.kv[l, z.pm:] = qkv[:, H:]
        queries = stack_heads(qkv[:, :H])
        q.q4[l] = queries
        scores = dot(queries, q.kv[l, :, :H], 1, 1) * 0.125
        scores = jnp.where(live, scores, -1000000000.0)
        e = jnp.exp(scores - jnp.max(scores, axis=-1, keepdims=True))
        rt = jnp.sum(e, axis=-1, keepdims=True)
        q.pexp[l] = e
        q.rtot[l] = rt
        own = fold_heads(dot(e.astype(BF), q.kv[l, :, H:]) / rt)
        q.att4[l] = own
        swap(q.atta.at[l, c], own.astype(BF), n_at[l])

    def attention_out(l):
        mine = at16(c * z.r, z.r)
        att = jnp.concatenate([q.atta[l, 0, mine], q.atta[l, 1, mine]], axis=1)
        after = q.xs[l] + dot(att, q.wo[l].reshape(z.inner, z.d))
        q.aft[l] = after
        xhat, _ = centre(after)
        gather_start(q.ffa.at[l], (xhat * vec(l, 4) + vec(l, 5)).astype(BF), n_ff[l])

    def hidden(l):
        h = dot(q.ffa[l].reshape(z.rows, z.d), w_up(l))
        q.hp[l] = h
        q.act[l] = (h * (0.5 * (1.0 + lax.erf(h * 0.7071067811865476)))).astype(BF)

    def down(l):
        scatter_sum(dot(q.act[l], w_dn(l)), l)

    def ff_back(l):
        gather_end(q.gza.at[l], n_gz[l])
        g = dot(q.gza[l].reshape(z.rows, z.d), w_dn(l), 1, 1)
        h = q.hp[l]
        slope = 0.5 * (1.0 + lax.erf(h * 0.7071067811865476)) + h * 0.3989422804014327 * jnp.exp(-0.5 * h * h)
        q.gpre[l] = (g * slope).astype(BF)
        scatter_sum(dot(q.gpre[l], w_up(l), 1, 1), L + l)

    def ff_grads(l):
        q.gdn[l] = dot(q.act[l], q.gza[l].reshape(z.rows, z.d), 0, 0).astype(BF).reshape(q.gdn.shape[1:])
        q.gup[l] = dot(q.ffa[l].reshape(z.rows, z.d), q.gpre[l], 0, 0).astype(BF).reshape(q.gup.shape[1:])

    def attn_back(l, gx):
        gff = scatter_end(L + l)
        xhat, rstd = centre(q.aft[l])
        q.gn[6 * l + 4] = jnp.sum(gff * xhat, axis=0)
        q.gn[6 * l + 5] = jnp.sum(gff, axis=0)
        gafter = gx + pull(xhat, rstd, gff, vec(l, 4))
        swap(q.gya.at[l, c], gafter.astype(BF), n_gy[l])
        gy = q.gya[l].reshape(z.latn, z.d)
        hb = z.blk[0] // 2
        wo_own = q.wo[l, pl.ds(c * hb, hb)].reshape(H, z.d)
        gatt = dot(gy, wo_own, 1, 1).astype(BF)
        g4 = stack_heads(gatt.astype(F32))
        delta = jnp.sum(g4 * stack_heads(q.att4[l]), axis=-1, keepdims=True)
        rt = q.rtot[l]
        e = q.pexp[l]
        gp = dot(g4.astype(BF), q.kv[l, :, H:], 1, 1)
        gs = (e / rt * (gp - delta)).astype(BF)
        gq = (fold_heads(dot(gs, q.kv[l, :, :H])) * 0.125).astype(BF)
        gk = (dot(gs, q.q4[l], 0, 0) * 0.125).astype(BF)
        gv = dot(e.astype(BF), (g4 / rt).astype(BF), 0, 0).astype(BF)
        glat = jnp.concatenate([gq, gk[z.pm:], gv[z.pm:]], axis=1)
        q.gl[l] = dot(glat, w_qkv(l), 1, 1).reshape(2, z.r, z.d)
        send(q.gl.at[l, 1 - c], q.grecv.at[l], sib, n_gl[l])
        q.gkvm[l, :, :H] = gk
        q.gkvm[l, :, H:] = gv
        arrive(q.grecv.at[l], n_gl[l])
        sent(q.grecv.at[l], n_gl[l])
        gln = q.gl[l, c] + q.grecv[l]
        xhat, rstd = centre(q.xs[l])
        q.gn[6 * l + 2] = jnp.sum(gln * xhat, axis=0)
        q.gn[6 * l + 3] = jnp.sum(gln, axis=0)
        return gafter + pull(xhat, rstd, gln, vec(l, 2)), gq

    def attn_grads(l, gq):
        to = q.gat.at[l]
        shape = (*z.blk, z.qrows)
        to[:, :, :, :, :H] = dot(q.mn[l, z.pm:], gq, 0, 0).astype(BF).reshape(*shape, H)
        to[:, :, :, :, H:3 * H] = dot(q.mn[l], q.gkvm[l], 0, 0).astype(BF).reshape(*shape, 2 * H)
        att = jnp.concatenate([q.atta[l, 0], q.atta[l, 1]], axis=1)
        cols = lanes(c * (z.d // 2), z.d // 2)
        gyc = jnp.concatenate([q.gya[l, 0, :, cols], q.gya[l, 1, :, cols]], axis=0)
        g = dot(att, gyc, 0, 0).astype(BF).reshape(*z.blk, z.orows, z.d // 2)
        to[:, :, :, :z.orows, 3 * H:] = g[..., :z.d // 4]
        to[:, :, :, z.orows:2 * z.orows, 3 * H:] = g[..., z.d // 4:]

    def media_back(l):
        q.cm[...] = dot(q.gkvm[l, :z.pm], w_kv(l), 1, 1)

        def piece(j, sums):
            rows = pl.ds(pl.multiple_of(j * z.pr, 8), z.pr)
            xhat, rstd = centre(q.media[j].astype(F32))
            cotm = q.cm[rows]
            add = cotm * vec(l, 0)
            q.macc[rows] = add if l == L - 1 else q.macc[rows] + add
            return sums[0] + col_sum(cotm * xhat), sums[1] + col_sum(cotm)

        zero = jnp.zeros((1, z.d), F32)
        u, v = lax.fori_loop(0, z.ns, piece, (zero, zero))
        q.gn[6 * l + 0] = u[0]
        q.gn[6 * l + 1] = v[0]

    if z.fused:
        n_ra, n_rb, n_rc, n_rf, n_ud, n_us, n_dd, n_ds = ([sem() for _ in range(L)] for _ in range(8))
        n_nd, n_ns = sem(), sem()

        def add_to(dst, x, w):
            dst[...] = (x[...].astype(F32) + w[...].astype(F32)).astype(BF)

        def grads_first(l):
            @pl.when(c == 0)
            def _():
                send(q.gat.at[l, :, :, 1 - y], q.ra.at[l], second, n_ra[l])

            @pl.when(c == 1)
            def _():
                send(q.gat.at[l, :, 1 - b], q.ra.at[l], second, n_ra[l])

        def grads_second(l):
            arrive(q.ra.at[l], n_ra[l])
            sent(q.ra.at[l], n_ra[l])

            @pl.when(c == 0)
            def _():
                add_to(q.sa.at[l], q.gat.at[l, :, :, y], q.ra.at[l])
                send(q.sa.at[l, :, 1 - b], q.rb.at[l], first, n_rb[l])

            @pl.when(c == 1)
            def _():
                add_to(q.sa.at[l], q.gat.at[l, :, b], q.ra.at[l])
                send(q.sa.at[l, :, 1 - y], q.rb.at[l], first, n_rb[l])

        def grads_third(l):
            arrive(q.rb.at[l], n_rb[l])
            sent(q.rb.at[l], n_rb[l])
            add_to(q.sb.at[l], q.sa.at[l, :, b * (1 - c) + y * c], q.rb.at[l])
            for t in range(1, za):
                o = (a + t) % za
                send(q.sb.at[l, o], q.rc.at[l, a], (o * 2 + b, s), n_rc[l])
            q.rc[l, a] = q.sb[l, a]

        def grads_last(l):
            part = q.rc.at[l, pl.ds(0, za - 1)]
            arrive(part, n_rc[l])
            sent(part, n_rc[l])
            v = q.rc[l, 0].astype(F32)
            for t in range(1, za):
                v = v + q.rc[l, t].astype(F32)
            q.sf[l] = v
            send(q.sf.at[l], q.rf.at[l], sib, n_rf[l])

        def grads_out(l):
            arrive(q.rf.at[l], n_rf[l])
            sent(q.rf.at[l], n_rf[l])
            for buf, cc in ((q.sf, c), (q.rf, 1 - c)):
                v = buf[l, at16(c * z.rq, z.rq), :3 * H]
                q.gq_out[l, :, lanes(cc * H, H)] = v[:, :H]
                q.gkv_out[l, :, lanes(cc * H, H)] = v[:, H:2 * H]
                q.gkv_out[l, :, lanes(z.inner + cc * H, H)] = v[:, 2 * H:]
                for part in range(2):
                    rows = at16(part * z.orows + c * z.ro, z.ro)
                    col = cc * (z.d // 2) + part * (z.d // 4)
                    q.go_out[l, :, lanes(col, z.d // 4)] = buf[l, rows, 3 * H:]

        def ff_pair(l):
            send(q.gup.at[l, :, 1 - c], q.updr.at[l], sib, n_ud[l])
            send(q.gdn.at[l, :, 1 - c], q.dndr.at[l], sib, n_dd[l])

        def ff_spread(l):
            arrive(q.dndr.at[l], n_dd[l])
            sent(q.dndr.at[l], n_dd[l])
            add_to(q.dns.at[l], q.gdn.at[l, :, c], q.dndr.at[l])
            for g in range(1, z.dp):
                o = (grp + g) % z.dp
                send(q.dns.at[l, o], q.dnr.at[l, grp], chip(o * TP + pos, c), n_ds[l])
            arrive(q.updr.at[l], n_ud[l])
            sent(q.updr.at[l], n_ud[l])
            add_to(q.ups.at[l], q.gup.at[l, :, c], q.updr.at[l])

            def one(t, _):
                kk = (k + t) % z.chips
                send(q.ups.at[l, kk], q.upr.at[l, k], chip(kk, c), n_us[l])
                return 0

            lax.fori_loop(1, z.chips, one, 0)
            q.dnr[l, grp] = q.dns[l, grp]
            q.upr[l, k] = q.ups[l, k]

        def ff_out(l):
            part = q.dnr.at[l, pl.ds(0, z.dp - 1)]
            arrive(part, n_ds[l])
            sent(part, n_ds[l])
            v = q.dnr[l, 0].astype(F32)
            for g in range(1, z.dp):
                v = v + q.dnr[l, g].astype(F32)
            q.gdn_out[l] = v
            part = q.upr.at[l, pl.ds(0, z.chips - 1)]
            arrive(part, n_us[l])
            sent(part, n_us[l])
            for p in range(TP):
                v = q.upr[l, p].astype(F32)
                for g in range(1, z.dp):
                    v = v + q.upr[l, g * TP + p].astype(F32)
                for g in range(z.dp):
                    col = (g * TP + p) * z.fc
                    q.gup_out[l, :, col:col + z.fc] = v[:, g * z.fc:(g + 1) * z.fc]

        def norms_pair():
            send(q.gn, q.gnd, sib, n_nd)

        def norms_spread():
            arrive(q.gnd, n_nd)
            sent(q.gnd, n_nd)
            q.gns[...] = q.gn[...] + q.gnd[...]

            def one(t, _):
                kk = (k + t) % z.chips
                dev = chip(kk, c)
                send(q.gns.at[:, lanes(dev[0] * z.lanes, z.lanes)], q.gnr.at[k], dev, n_ns)
                return 0

            lax.fori_loop(1, z.chips, one, 0)
            q.gnr[k] = q.gns[:, lanes(i * z.lanes, z.lanes)]

        def norms_out():
            part = q.gnr.at[pl.ds(0, z.chips - 1)]
            arrive(part, n_ns)
            sent(part, n_ns)
            v = q.gnr[0]
            for t in range(1, z.chips):
                v = v + q.gnr[t]
            q.gn_out[...] = v
    else:
        def grads_first(l):
            pltpu.make_async_copy(q.gat.at[l], q.gat_out.at[l], ls.at[9 + l]).start()

        def grads_out(l):
            pltpu.make_async_copy(q.gat.at[l], q.gat_out.at[l], ls.at[9 + l]).wait()

        def ff_pair(l):
            pltpu.make_async_copy(q.gup.at[l], q.gup_out.at[l], ls.at[11 + l]).start()
            pltpu.make_async_copy(q.gdn.at[l], q.gdn_out.at[l], ls.at[13 + l]).start()

        def ff_out(l):
            pltpu.make_async_copy(q.gup.at[l], q.gup_out.at[l], ls.at[11 + l]).wait()
            pltpu.make_async_copy(q.gdn.at[l], q.gdn_out.at[l], ls.at[13 + l]).wait()

        grads_second = grads_third = grads_last = ff_spread = nothing

        def norms_pair():
            pass

        def norms_spread():
            pass

        def norms_out():
            q.gn_out[...] = q.gn[...]

    for l in range(L):
        weights_pair(l)
    rows_start()
    norms_start()
    weights_z(0)
    arrive(q.lc, n_lc)
    cot = q.lc[:, 1].astype(F32).reshape(z.r, z.d)
    q.xs[0] = q.lc[:, 0].astype(F32).reshape(z.r, z.d)
    norms_end()
    media_share()
    weights_first(0)
    weights_ff(0)
    arrive(q.media.at[pl.ds(0, z.ny)], n_mb)
    lax.fori_loop(0, z.ns, norm_piece, 0)
    weights_second(0)
    gather_start(q.gza.at[L - 1], cot.astype(BF), n_gz[L - 1])
    weights_qkv_end(0)
    media_kv(0)
    for l in range(L):
        if l + 1 < L:
            weights_z(l + 1)
        attention(l)
        weights_out_share(l)
        weights_out_end(l)
        attention_out(l)
        weights_ff_share(l)
        if l + 1 < L:
            weights_first(l + 1)
            weights_ff(l + 1)
        weights_ff_end(l)
        gather_end(q.ffa.at[l], n_ff[l])
        hidden(l)
        if l + 1 < L:
            down(l)
            weights_second(l + 1)
            q.xs[l + 1] = q.aft[l] + scatter_end(l)
            weights_qkv_end(l + 1)
            media_kv(l + 1)
    gx = cot
    for l in reversed(range(L)):
        if l < L - 1:
            gather_start(q.gza.at[l], gx.astype(BF), n_gz[l])
            attn_grads(l + 1, gq)
            grads_first(l + 1)
            media_back(l + 1)
            q.xout[...] = (q.aft[L - 1] + scatter_end(L - 1)).astype(z.lt).reshape(z.ny, z.lr, z.d)
        ff_back(l)
        if l == L - 1:
            down(l)
        ff_grads(l)
        ff_pair(l)
        if l < L - 1:
            ff_spread(l + 1)
            grads_second(l + 1)
        gx, gq = attn_back(l, gx)
    attn_grads(0, gq)
    grads_first(0)
    for l in range(1, L):
        grads_third(l)
    ff_spread(0)
    q.gxo[...] = gx.reshape(z.ny, z.lr, z.d)

    def give_back(srcs, out, n):
        for j in range(z.ny):
            to = c * z.ny + j

            @pl.when(to != s)
            def _():
                send(srcs[j], out.at[y], (i, to), n)

            @pl.when(to == s)
            def _():
                keep(srcs[j], out.at[y], n)

    give_back([q.xout.at[j] for j in range(z.ny)], q.lat_out, n_lo)
    give_back([q.gxo.at[j] for j in range(z.ny)], q.glat_out, n_go)
    media_back(0)
    norms_pair()
    h = z.pm // 2
    q.msend[...] = q.macc[at16((1 - c) * h, h)].astype(z.mt)
    send(q.msend, q.mrecv, sib, n_md)
    grads_second(0)
    for l in range(1, L):
        grads_last(l)
    norms_spread()
    arrive(q.mrecv, n_md)
    sent(q.mrecv, n_md)
    xhat, rstd = centre(q.media[pl.ds(c * z.ny, z.ny)].astype(F32).reshape(h, z.d))
    gm = pull(xhat, rstd, q.macc[at16(c * h, h)] + q.mrecv[...].astype(F32), jnp.ones((1, z.d), F32))
    mo = q.mn.at[0] if z.mt == BF else q.cm
    for j in range(z.ny):
        mo[j * z.pr:(j + 1) * z.pr] = gm[j * z.pr:(j + 1) * z.pr].astype(z.mt)
    srcs = [mo.at[pl.ds(j * z.pr, z.pr)] for j in range(z.ny)]
    give_back(srcs, q.gmedia_out, n_mo)
    grads_third(0)
    for l in range(1, L):
        grads_out(l)
        ff_out(l)
    ff_out(0)
    norms_out()
    grads_last(0)
    grads_out(0)
    arrive(q.lat_out, n_lo)
    arrive(q.glat_out, n_go)
    arrive(q.gmedia_out, n_mo)
    rows_sent()
    for j in range(z.ny):
        @pl.when(c * z.ny + j != s)
        def _():
            gone(q.xout.at[0], n_lo)
            gone(q.gxo.at[0], n_go)
            gone(srcs[0], n_mo)
    if z.fused:
        part = q.nrecv.at[pl.ds(0, z.ni - 1)]
        rest = q.nrecv.at[0, pl.ds(0, z.ns - 1)]
        gone(part, n_nrm)
        gone(rest, n_nrm)
    for ref, n in waits:
        gone(ref, n)


def call(z, *args):
    ins, outs, scratch = inputs_of(z), outputs_of(z), scratch_of(z)
    names = [n for n, _ in ins] + list(outs) + list(scratch)
    got = pl.pallas_call(
        functools.partial(kernel, z, names),
        out_shape=[jax.ShapeDtypeStruct(s, d) for _, s, d in outs.values()],
        in_specs=[pl.BlockSpec(memory_space=m) for _, m in ins],
        out_specs=[pl.BlockSpec(memory_space=m) for m, _, _ in outs.values()],
        scratch_shapes=list(scratch.values()),
        compiler_params=pltpu.CompilerParams(collective_id=0, has_side_effects=True, vmem_limit_bytes=62 * 2**20),
    )(*args)
    return types.SimpleNamespace(**dict(zip(outs, got)))


def body(mesh, media, latents, counts, wq, wkv, wout, wup, wdown, norms, cotangent):
    z = Sizes(mesh, media, latents, wq, wkv, wout, wup, wdown)
    L, D, H = z.layers, z.d, z.half
    i, s = lax.axis_index("img"), lax.axis_index("seq")
    y, c = s // 2, s % 2
    k = i * z.ny + y
    pos = k % TP
    latcot = jnp.stack([latents, cotangent], axis=1).astype(z.lt)
    media = media.astype(z.mt)
    own = norms.reshape(6 * L, -1)
    if z.fused:
        width = own.shape[1]
        tile = jnp.zeros((16, z.lanes), own.dtype)
        tile = lax.dynamic_update_slice(tile, own, (0, s * width))
        o = call(z, media, latcot, counts, tile, wq, wkv, wout, wup, wdown)
        gn = lax.dynamic_slice(o.gn_out, (0, s * width), (6 * L, width)).reshape(L, 6, width)
        return (o.lat_out.astype(BF), o.gmedia_out.astype(F32), o.glat_out, o.gq_out, o.gkv_out, o.go_out,
                o.gup_out, o.gdn_out, gn)

    def pick(v, axis, index):
        return lax.dynamic_index_in_dim(v, index, axis, keepdims=False)

    def gather(v, axis):
        return lax.all_gather(v, BOTH, axis=axis, tiled=True)

    nrm = jnp.pad(gather(own, 1).astype(F32), ((0, 16 - 6 * L), (0, 0)))
    fq = pick(gather(wq, 1).reshape(L, D, 2, H), 2, c)
    fkv = pick(gather(wkv, 1).reshape(L, D, 2, 2, H), 3, c).reshape(L, D, 2 * H)
    wqkv = jnp.concatenate([fq, fkv], axis=2).reshape(L, *z.blk, z.qrows, 3 * H)
    wo = gather(wout, 1).reshape(L, *z.blk, 2, z.orows // 2, D)
    fup = pick(gather(wup, 1).reshape(L, D, z.dp, TP, z.fc), 3, pos).reshape(L, 1, 2, D // 2, z.fs)
    fdn = pick(gather(wdown, 1).reshape(L, z.dp, TP, z.fc, D), 2, pos).reshape(L, 1, 2, z.fs // 2, D)
    o = call(z, media, latcot, counts, nrm, wqkv, wo, fup, fdn)

    def spread(g, shape, axis, index):
        return lax.dynamic_update_index_in_dim(jnp.zeros(shape, F32), g.astype(F32), index, axis)

    def scatter(g):
        return lax.psum_scatter(g, BOTH, scatter_dimension=1, tiled=True)

    gat = o.gat_out.reshape(L, z.nblk, z.qrows, z.wide)
    gout = jnp.concatenate([gat[:, :, : z.orows, 3 * H :], gat[:, :, z.orows : 2 * z.orows, 3 * H :]], axis=3)
    gout = gout.reshape(L, z.inner, D // 2)
    gat = gat.reshape(L, D, z.wide)
    gq = scatter(spread(gat[:, :, :H], (L, D, 2, H), 2, c).reshape(L, D, z.inner))
    gkv = spread(gat[:, :, H : 3 * H].reshape(L, D, 2, H), (L, D, 2, 2, H), 3, c)
    gkv = scatter(gkv.reshape(L, D, 2 * z.inner))
    go = scatter(spread(gout, (L, z.inner, 2, D // 2), 2, c).reshape(L, z.inner, D))
    gu = spread(o.gup_out.reshape(L, D, z.dp, z.fc), (L, D, z.dp, TP, z.fc), 3, pos)
    gu = scatter(gu.reshape(L, D, z.ff))
    gd = spread(o.gdn_out.reshape(L, z.dp, z.fc, D), (L, z.dp, TP, z.fc, D), 2, pos)
    gd = scatter(gd.reshape(L, z.ff, D))
    gn = lax.psum_scatter(o.gn_out, BOTH, scatter_dimension=1, tiled=True)[: 6 * L].reshape(L, 6, -1)
    return o.lat_out.astype(BF), o.gmedia_out.astype(F32), o.glat_out, gq, gkv, go, gu, gd, gn


def solution(mesh):
    rows = P("img", "seq", None)
    weight = P(None, BOTH, None)
    return jax.shard_map(
        functools.partial(body, mesh),
        mesh=mesh,
        in_specs=(rows, rows, P("img"), weight, weight, weight, weight, weight, P(None, None, BOTH), rows),
        out_specs=(rows, rows, rows, weight, weight, weight, weight, weight, P(None, None, BOTH)),
        check_vma=False,
    )
```

time: 1850 us -> 219 us (0.12); the launches traced: 1820 us -> 219 us
  waiting for transfers between devices: 1200 us -> 0 us
  local copies, waits for them, and re-layouts: 443 us -> 8.03 us
  Pallas kernels: 110 us -> 206 us
  blocking collectives: 37.8 us -> 0 us
    reduce_scatter x5 -> x0, waiting for transfers between devices: 894 us -> none  [body(): scat = lambda g: lax.psum_scatter(g, BOTH, scatter_dimension=1, tiled=True)]
    all_gather x5 -> x0, waiting for transfers between devices: 304 us -> none  [body(): gather = lambda a, axis: lax.all_gather(a, BOTH, axis=axis, tiled=True)]
    dynamic_update_slice x4 -> x1, local copies, waits for them, and re-layouts: 256 us -> 0.62 us  [body(): tile = lax.dynamic_update_slice(tile, own, (0, s * width))]
    pallas_call x1, Pallas kernels: 110 us -> 206 us  [call(): pl.pallas_call(functools.partial(kernel, z, names), out_shape=[jax.ShapeD...]
    reshape x10 -> x2, local copies, waits for them, and re-layouts: 76.8 us -> 0.02 us  [the longest x1 0.02 us: body(): own = norms.reshape(6 * L, -1)]
    broadcast_in_dim x7 -> x1, local copies, waits for them, and re-layouts: 38.5 us -> 0.01 us  [body(): tile = jnp.zeros((16, z.lanes), own.dtype)]
    all_gather x1 -> x0, blocking collectives: 37.8 us -> none  [body(): gather = lambda a, axis: lax.all_gather(a, BOTH, axis=axis, tiled=True)]
    dynamic_slice x4 -> x1, local copies, waits for them, and re-layouts: 37.5 us -> 0.83 us  [body(): lax.dynamic_slice(o.gn_out, (0, s * width), (6 * L, width))]
  transfers between devices with their start and end apart: 11 -> 0, of which waited for: 9 -> 0; matrix products, arithmetic and copies ran while one was open for 25% -> 0% of each run, Pallas kernels for 0% -> 0%
where the time goes in v2:
time: 219 us
  Pallas kernels  206 us (94%)
  local copies, waits for them, and re-layouts  8.03 us (4%)
  other arithmetic  3.86 us (2%)
    pallas_call x1, Pallas kernels, call(): pl.pallas_call(functools.partial(kernel, z, names), out_shape=[jax.ShapeD...  206 us
    unnamed x25, local copies, waits for them, and re-layouts  6.56 us

profile of v2, /device:TPU:9, one launch (start us, length us, event | category | flops | bytes accessed | tf_op | source)
XLA Modules:
  0.0 218.6 jit_solution(12688841031665389922)
XLA Ops:
  0.6 0.7 copy.20
  1.4 0.6 dynamic_update_slice.3.refs_3_
  2.0 0.0 copy-start.7
  2.0 1.5 pad_maximum_fusion.refs_1_
  3.5 0.0 copy-done.7
  3.5 206.0 %shard_map.169 = (bf16[2,16,1024]{2,1,0:T(8,128)(2,1)}, bf16[2,144,1024]{2,1,0:T(8,128)(2,1)}, f32[2,16,1024]{2,1,0:T(8,128)}, f32[2,32,512]{2,1,0:T(8,128)}, f3...) custom-call(bf16[2,144,1024]{2,1,0:T(8,128)(2,1)} %refs_0_.1, ...), custom_call_target="tpu_custom_call" | custom-call | tf_op jit(solution)/shard_map/pallas_call | solution.py:899
  209.5 0.0 copy-start.6
  209.6 0.0 copy-start.5
  209.6 0.0 copy-start.4
  209.6 0.8 constant_dynamic-slice_fusion
  210.4 0.6 copy.21
  211.0 2.3 %convert_element_type.3 = f32[2,144,1024]{2,1,0:T(8,128)} convert(bf16[2,144,1024]{2,1,0:T(8,128)(2,1)} %get-tuple-element.19) | non-fusion elementwise | flops 294912 | bytes 1769472 | tf_op jit(solution)/shard_map/convert_element_type | solution.py:926
  213.3 0.0 copy-done.6
  213.3 0.6 copy.30
  214.0 0.0 copy-done.5
  214.0 0.7 copy.31
  214.6 0.0 copy-done.4
  214.6 0.7 copy.32
  215.3 0.0 copy-done.2
  215.3 0.7 copy.33
  216.0 0.0 copy-done.3
  216.0 0.7 copy.34
  216.7 1.0 copy.35
  217.6 1.0 copy.36
  (9 shorter events, 0.0 us)
Async XLA Ops:
  2.0 1.6 copy-start.7
  209.5 3.8 %copy-start.6 = (bf16[2,16,1024]{2,1,0:T(8,128)(2,1)S(1)}, bf16[2,16,1024]{2,1,0:T(8,128)(2,1)}, u32[]{:S(2)}) copy-start(bf16[2,16,1024]{2,1,0:T(8,128)(2,1)} %get-tuple-element.45) | copy-start | bytes 196612
  209.6 4.4 %copy-start.5 = (f32[2,16,1024]{2,1,0:T(8,128)S(1)}, f32[2,16,1024]{2,1,0:T(8,128)}, u32[]{:S(2)}) copy-start(f32[2,16,1024]{2,1,0:T(8,128)} %get-tuple-element.47) | copy-start | bytes 393220
  209.6 5.1 %copy-start.4 = (f32[2,32,512]{2,1,0:T(8,128)S(1)}, f32[2,32,512]{2,1,0:T(8,128)}, u32[]{:S(2)}) copy-start(f32[2,32,512]{2,1,0:T(8,128)} %get-tuple-element.48) | copy-start | bytes 393220
  211.0 4.3 %copy-start.2 = (f32[2,32,1024]{2,1,0:T(8,128)S(1)}, f32[2,32,1024]{2,1,0:T(8,128)}, u32[]{:S(2)}) copy-start(f32[2,32,1024]{2,1,0:T(8,128)} %get-tuple-element.49) | copy-start | bytes 786436
  211.0 5.0 %copy-start.3 = (f32[2,16,1024]{2,1,0:T(8,128)S(1)}, f32[2,16,1024]{2,1,0:T(8,128)}, u32[]{:S(2)}) copy-start(f32[2,16,1024]{2,1,0:T(8,128)} %get-tuple-element.50) | copy-start | bytes 393220
  211.0 5.6 %copy-start.1 = (f32[2,32,4096]{2,1,0:T(8,128)S(1)}, f32[2,32,4096]{2,1,0:T(8,128)}, u32[]{:S(2)}) copy-start(f32[2,32,4096]{2,1,0:T(8,128)} %get-tuple-element.51) | copy-start | bytes 3145732
  216.0 1.6 copy-start

commit v3 on v2

v3 whole, which is shorter than its diff:
```python
import functools
import types

import jax
import jax.numpy as jnp
from jax import lax
from jax.experimental import pallas as pl
from jax.experimental.pallas import tpu as pltpu
from jax.sharding import PartitionSpec as P

HEAD = 64
EPS = 1e-05
MESH = pl.DeviceIdType.MESH
BF = jnp.bfloat16
F32 = jnp.float32
TP = 8
BOTH = ("img", "seq")


class Sizes:
    def __init__(self, mesh, media, latents, wq, wkv, wout, wup, wdown):
        self.ni, self.ns = mesh.shape["img"], mesh.shape["seq"]
        self.ny = self.ns // 2
        self.chips = self.ni * self.ny
        self.layers = wq.shape[0]
        self.d = media.shape[2]
        self.nimg, self.pr = media.shape[0], media.shape[1]
        self.lr = latents.shape[1]
        self.inner = wq.shape[2]
        self.half = self.inner // 2
        self.ff = wup.shape[2]
        self.fs = self.ff // TP
        self.dp = self.chips // TP
        self.fc = self.ff // self.chips
        self.pm = self.pr * self.ns
        self.latn = self.lr * self.ns
        self.r = self.latn // 2
        self.keys = self.pm + self.latn
        self.heads = self.half // HEAD
        self.rows = TP * self.r
        self.mt = BF if self.pr % 16 == 0 else F32
        self.lt = BF if self.lr % 16 == 0 else F32
        self.rq, self.ro, self.rd = wq.shape[1], wout.shape[1], wdown.shape[1]
        self.lanes = self.d // self.ni
        whole_tiles = all(v % 16 == 0 for v in (self.rq, self.ro, self.rd))
        whole_tiles = whole_tiles and self.fc % 128 == 0 and self.lanes % 128 == 0
        self.fused = whole_tiles and self.ny == 2 == self.layers and self.ni % 4 == 0
        self.blk = (self.ni // 2, 2, self.ny) if self.fused else (2, 1, 1)
        self.nblk = self.blk[0] * self.blk[1] * self.blk[2]
        self.qrows = self.d // self.nblk
        self.orows = self.inner // self.nblk
        self.quart = self.d // 4
        assert self.nimg == self.ny and TP % self.ny == 0


def dot(a, b, ca=1, cb=0):
    return lax.dot_general(a, b, (((ca,), (cb,)), ((), ())), preferred_element_type=F32)


def centre(v):
    c = v - jnp.mean(v, axis=-1, keepdims=True)
    rstd = lax.rsqrt(jnp.mean(c * c, axis=-1, keepdims=True) + EPS)
    return c * rstd, rstd


def pull(xhat, rstd, cot, gain):
    g = cot * gain
    m1 = jnp.mean(g, axis=-1, keepdims=True)
    m2 = jnp.mean(g * xhat, axis=-1, keepdims=True)
    return rstd * (g - m1 - xhat * m2)


def col_sum(v):
    return jnp.sum(v, axis=0, keepdims=True)


def inputs_of(z):
    names = ["media_in", "lat_in", "cot_in", "counts", "nrm_in"]
    if z.fused:
        names += ["wq_in", "wkv_in", "wo_in", "wup_in", "wdn_in"]
    else:
        names += ["wq_in", "wk_in", "wv_in", "wo_in", "wup_in", "wdn_in"]
    return [(n, pltpu.SMEM if n == "counts" else pl.ANY) for n in names]


def outputs_of(z):
    L, D = z.layers, z.d
    outs = dict(
        lat_out=((z.ny, z.lr, D), z.lt),
        gmedia_out=((z.ny, z.pr, D), z.mt),
        glat_out=((z.ny, z.lr, D), F32),
    )
    if z.fused:
        outs.update(
            qs_out=((L, 3, 2, z.rq, z.half), F32),
            os_out=((L, 2, 2, z.ro, z.quart), F32),
            upr=((L, z.chips, z.rq, z.fs), BF),
            dnr=((L, z.dp, z.rd, D), BF),
            gnr=((z.chips, 16, z.lanes), F32),
        )
    else:
        outs.update(
            gaq_out=((L, *z.blk, z.qrows, z.half), BF),
            gak_out=((L, *z.blk, z.qrows, z.half), BF),
            gav_out=((L, *z.blk, z.qrows, z.half), BF),
            gao_out=((L, *z.blk, 2 * z.orows, z.quart), BF),
            gup_out=((L, 1, 2, D // 2, z.fs), BF),
            gdn_out=((L, 1, 2, z.fs // 2, D), BF),
            gn_out=((16, D), F32),
        )
    return outs


def scratch_of(z):
    L, D, R, T = z.layers, z.d, z.r, TP
    kq = z.heads * z.latn
    cu = z.chips if z.fused else 1
    gd = z.dp if z.fused else 1
    v = dict(
        media=((z.ns, z.pr, D), z.mt),
        lc=((2, z.ny, z.lr, D), z.lt),
        mn=((L, z.keys, D), BF),
        kv=((L, z.keys, 2 * z.half), BF),
        wq=((L, *z.blk, z.qrows, z.half), BF),
        wk=((L, *z.blk, z.qrows, z.half), BF),
        wv=((L, *z.blk, z.qrows, z.half), BF),
        wo=((L, *z.blk, 2, z.orows // 2, D), BF),
        wup=((L, cu, 2, D // (2 * cu), z.fs), BF),
        wdn=((L, gd, 2, z.fs // (2 * gd), D), BF),
        nrm=((16, D), F32),
        q4=((L, kq, z.half), BF),
        pexp=((L, kq, z.keys), F32),
        rtot=((L, kq, 1), F32),
        att4=((L, z.latn, z.half), F32),
        atta=((L, 2, z.latn, z.half), BF),
        aft=((L, R, D), F32),
        ffa=((L, T, R, D), BF),
        hp=((L, z.rows, z.fs), F32),
        act=((L, z.rows, z.fs), BF),
        xs=((L, R, D), F32),
        gza=((L, T, R, D), BF),
        psend=((2 * L, T, R, D), BF),
        precv=((2 * L, T, R, D), BF),
        gpre=((L, z.rows, z.fs), BF),
        gya=((L, 2, R, D), BF),
        gl=((L, 2, R, D), F32),
        grecv=((L, R, D), F32),
        gkvm=((L, z.keys, 2 * z.half), BF),
        macc=((z.pm, D), F32),
        msend=((z.pm // 2, D), z.mt),
        mrecv=((z.pm // 2, D), z.mt),
        gn=((16, D), F32),
        xout=((z.ny, z.lr, D), z.lt),
        gxo=((z.ny, z.lr, D), F32),
        cm=((z.pm, D), F32),
        fold=((kq, z.half), F32),
        gak=((L, *z.blk, z.qrows, z.half), BF),
        gav=((L, *z.blk, z.qrows, z.half), BF),
        gaq=((L, *z.blk, z.qrows, z.half), BF),
        gao=((L, *z.blk, 2 * z.orows, z.quart), BF),
        gup=((L, cu, 2, D // (2 * cu), z.fs), BF),
        gdn=((L, gd, 2, z.fs // (2 * gd), D), BF),
    )
    if z.fused:
        za = z.blk[0]
        v.update(
            ntile=((16, z.lanes), BF),
            npair=((16, z.lanes), BF),
            nrecv=((z.chips, 16, z.lanes), BF),
            updr=((L, z.chips, z.rq, z.fs), BF),
            ups=((L, z.chips, z.rq, z.fs), BF),
            dndr=((L, z.dp, z.rd, D), BF),
            dns=((L, z.dp, z.rd, D), BF),
            gns=((16, D), F32),
            gnd=((16, D), F32),
        )
        for part in "kvqo":
            rows, cols = (2 * z.orows, z.quart) if part == "o" else (z.qrows, z.half)
            v["ra" + part] = ((L, za, 2, rows, cols), BF)
            v["sa" + part] = ((L, za, 2, rows, cols), BF)
            v["rb" + part] = ((L, za, rows, cols), BF)
            v["sb" + part] = ((L, za, rows, cols), BF)
            v["rc" + part] = ((L, za, rows, cols), BF)
            v["sf" + part] = ((L, rows, cols), F32)
    out = {n: pltpu.VMEM(s, d) for n, (s, d) in v.items()}
    out.update(ss=pltpu.SemaphoreType.DMA((NSEM,)), rs=pltpu.SemaphoreType.DMA((NSEM,)), ls=pltpu.SemaphoreType.DMA((32,)))
    return out


NSEM = 160


def kernel(z, names, *refs):
    L = z.layers
    q = types.SimpleNamespace(**dict(zip(names, refs)))
    ss, rs, ls = q.ss, q.rs, q.ls
    i = lax.axis_index("img")
    s = lax.axis_index("seq")
    y, c = s // 2, s % 2
    k = i * z.ny + y
    pos, grp = k % TP, k // TP
    sib = (i, y * 2 + (1 - c))
    a, b = i // 2, i % 2

    def chip(kk, cc):
        return (kk // z.ny, (kk % z.ny) * 2 + cc)

    def peer(t):
        return chip(grp * TP + (pos + t) % TP, c)

    waits = []
    used = [0]

    def sem():
        used[0] += 1
        return used[0] - 1

    def send(src, dst, dev, n):
        pltpu.make_async_remote_copy(src, dst, ss.at[n], rs.at[n], device_id=dev, device_id_type=MESH).start()

    def send_by_core(src0, dst0, src1, dst1, dev, n):
        @pl.when(c == 0)
        def _():
            send(src0, dst0, dev, n)

        @pl.when(c == 1)
        def _():
            send(src1, dst1, dev, n)

    def keep(src, dst, n):
        pltpu.make_async_copy(src, dst, rs.at[n]).start()

    def arrive(ref, n):
        pltpu.make_async_copy(ref, ref, rs.at[n]).wait()

    def gone(ref, n):
        pltpu.make_async_copy(ref, ref, ss.at[n]).wait()

    def sent(ref, n):
        waits.append((ref, n))

    bar = pltpu.get_barrier_semaphore()

    def greet(dev):
        pl.semaphore_signal(bar, inc=1, device_id=dev, device_id_type=MESH)

    def greet_chip(t, _):
        greet(chip((k + t) % z.chips, c))
        return 0

    greet(sib)
    for t in range(1, z.ny):
        greet((i, ((y + t) % z.ny) * 2 + (1 - c)))
    lax.fori_loop(1, z.chips, greet_chip, 0)
    pl.semaphore_wait(bar, z.chips - 1 + z.ny)

    def lanes(start, size):
        return pl.ds(pl.multiple_of(start, 128), size)

    def at16(start, size):
        return pl.ds(pl.multiple_of(start, 16), size)

    H = z.half
    if z.fused:
        za = z.blk[0]
        n_w0, n_w1, n_w2, n_w3 = ({p: [sem() for _ in range(L)] for p in "kvqo"} for _ in range(4))
        n_od = [sem() for _ in range(L)]
        n_ua, n_ub, n_da, n_db = ([sem() for _ in range(L)] for _ in range(4))
        n_np, n_nrm = sem(), sem()
        xdev = (i + 1 - 2 * b, s)
        ydev = (i, (1 - y) * 2 + c)
        first = (xdev[0] * (1 - c) + i * c, s * (1 - c) + ydev[1] * c)
        second = (i * (1 - c) + xdev[0] * c, ydev[1] * (1 - c) + s * c)
        bufs = dict(k=q.wk, v=q.wv, q=q.wq)

        def block(p, l, *at):
            if p == "o":
                return q.wo.at[(l, *at, *(slice(None),) * (3 - len(at)), c)]
            return bufs[p].at[(l, *at)]

        def weights_pair(l):
            rows = at16(c * z.rq, z.rq)
            for cc, dev in ((1 - c, sib), (c, None)):
                for p, src in (
                    ("k", q.wkv_in.at[l, :, lanes(cc * H, H)]),
                    ("v", q.wkv_in.at[l, :, lanes(z.inner + cc * H, H)]),
                    ("q", q.wq_in.at[l, :, lanes(cc * H, H)]),
                ):
                    dst = bufs[p].at[l, a, b, y, rows]
                    if dev is None:
                        keep(src, dst, n_w0[p][l])
                    else:
                        send(src, dst, dev, n_w0[p][l])
            for p in "kvq":
                sent(q.wq.at[l, 0, 0, 0, pl.ds(0, z.rq)], n_w0[p][l])
            keep(q.wo_in.at[l], q.wo.at[l, a, b, y, c], n_w0["o"][l])

        def weights_z(l, parts):
            for p in parts:
                own = block(p, l, a, b, y)
                arrive(own, n_w0[p][l])
                for t in range(1, za):
                    send(own, own, (((a + t) % za) * 2 + b, s), n_w1[p][l])

        def weights_first(l, parts):
            for p in parts:
                got = block(p, l, pl.ds(0, za - 1), 0, 0)
                arrive(got, n_w1[p][l])
                sent(got, n_w1[p][l])
                own = block(p, l, slice(None), b, y)
                send(own, own, first, n_w2[p][l])

        def weights_second(l, parts):
            for p in parts:
                got = block(p, l, slice(None), 0, 0)
                arrive(got, n_w2[p][l])
                sent(got, n_w2[p][l])
                ref0, ref1 = block(p, l, slice(None), slice(None), y), block(p, l, slice(None), b)
                send_by_core(ref0, ref0, ref1, ref1, second, n_w3[p][l])

        def weights_end(l, parts):
            for p in parts:
                got = block(p, l, slice(None), 0)
                arrive(got, n_w3[p][l])
                sent(got, n_w3[p][l])
                if p == "o":
                    ref = block(p, l)
                    send(ref, ref, sib, n_od[l])

        def weights_out_end(l):
            ref = q.wo.at[l, :, :, :, 0]
            arrive(ref, n_od[l])
            sent(ref, n_od[l])

        def weights_ff(l):
            def one(t, _):
                kk = (k + t) % z.chips
                dev = chip(kk, c)
                for g in range(z.dp):
                    src = q.wup_in.at[l, :, lanes((g * TP + kk % TP) * z.fc, z.fc)]
                    send(src, q.wup.at[l, k, c, :, pl.ds(g * z.fc, z.fc)], dev, n_ua[l])
                return 0

            for g in range(1, z.dp):
                dev = chip(((grp + g) % z.dp) * TP + pos, c)
                send(q.wdn_in.at[l], q.wdn.at[l, grp, c], dev, n_da[l])
            keep(q.wdn_in.at[l], q.wdn.at[l, grp, c], n_da[l])
            lax.fori_loop(1, z.chips, one, 0)
            for g in range(z.dp):
                src = q.wup_in.at[l, :, lanes((g * TP + pos) * z.fc, z.fc)]
                keep(src, q.wup.at[l, k, c, :, pl.ds(g * z.fc, z.fc)], n_ua[l])
            sent(q.wup.at[l, pl.ds(0, z.chips - 1), 0], n_ua[l])
            sent(q.wdn.at[l, pl.ds(0, z.dp - 1), 0], n_da[l])

        def weights_ff_share(l):
            arrive(q.wup.at[l, :, 0], n_ua[l])
            send(q.wup.at[l, :, c], q.wup.at[l, :, c], sib, n_ub[l])
            arrive(q.wdn.at[l, :, 0], n_da[l])
            send(q.wdn.at[l, :, c], q.wdn.at[l, :, c], sib, n_db[l])

        def weights_ff_end(l):
            arrive(q.wup.at[l, :, 0], n_ub[l])
            sent(q.wup.at[l, :, 0], n_ub[l])
            arrive(q.wdn.at[l, :, 0], n_db[l])
            sent(q.wdn.at[l, :, 0], n_db[l])

        def norms_start():
            send(q.nrm_in, q.ntile, sib, n_np)
            pltpu.make_async_copy(q.nrm_in, q.npair, ls.at[0]).start()

        def norms_spread_in():
            pltpu.make_async_copy(q.nrm_in, q.npair, ls.at[0]).wait()
            arrive(q.ntile, n_np)
            sent(q.ntile, n_np)
            q.nrecv[k] = q.npair[...] + q.ntile[...]

            def one(t, _):
                send(q.nrecv.at[k], q.nrecv.at[k], chip((k + t) % z.chips, c), n_nrm)
                return 0

            lax.fori_loop(1, z.chips, one, 0)

        def norms_end():
            part = q.nrecv.at[pl.ds(0, z.chips - 1)]
            arrive(part, n_nrm)
            sent(part, n_nrm)
            for ii in range(z.ni):
                v = q.nrecv[ii * z.ny].astype(F32)
                for j in range(1, z.ny):
                    v = v + q.nrecv[ii * z.ny + j].astype(F32)
                q.nrm[:, ii * z.lanes:(ii + 1) * z.lanes] = v
    else:
        loads = [(q.nrm_in, q.nrm)]
        for l in range(L):
            loads += [(getattr(q, n + "_in").at[l], getattr(q, n).at[l]) for n in ("wk", "wq", "wo", "wup", "wdn", "wv")]

        def norms_start():
            for n, (src, dst) in enumerate(loads):
                pltpu.make_async_copy(src, dst, ls.at[n]).start()

        def load_end(n):
            pltpu.make_async_copy(*loads[n], ls.at[n]).wait()

        def norms_spread_in():
            pass

        def norms_end():
            load_end(0)

        def nothing(l, parts=None):
            pass

        weights_pair = weights_z = weights_first = weights_second = nothing
        weights_ff = weights_ff_share = nothing

        def weights_end(l, parts):
            for p in parts:
                if p != "o":
                    load_end(1 + 6 * l + dict(k=0, q=1, v=5)[p])

        def weights_out_end(l):
            load_end(3 + 6 * l)

        def weights_ff_end(l):
            load_end(4 + 6 * l)
            load_end(5 + 6 * l)

    def w_q(l):
        return q.wq[l].reshape(z.d, H)

    def w_k(l):
        return q.wk[l].reshape(z.d, H)

    def w_v(l):
        return q.wv[l].reshape(z.d, H)

    def w_up(l):
        return q.wup[l].reshape(z.d, z.fs)

    def w_dn(l):
        return q.wdn[l].reshape(z.fs, z.d)

    n_la, n_lb, n_ma, n_mb = sem(), sem(), sem(), sem()
    n_ff, n_gz, n_ln, n_at, n_gy, n_gl = ([sem() for _ in range(L)] for _ in range(6))
    n_rs = [sem() for _ in range(2 * L)]
    n_md, n_lo, n_go, n_mo = sem(), sem(), sem(), sem()
    own_slot = s % z.ny

    def rows_start():
        for t in range(1, z.ny):
            yy = (y + t) % z.ny
            send(q.media_in.at[yy], q.media.at[s], (i, yy * 2 + c), n_ma)
        keep(q.media_in.at[y], q.media.at[s], n_ma)
        send(q.media_in.at[y], q.media.at[s], sib, n_mb)
        for yy in range(z.ny):
            to = yy * 2 + s // z.ny

            @pl.when(to != s)
            def _():
                send(q.lat_in.at[yy], q.lc.at[0, own_slot], (i, to), n_la)
                send(q.cot_in.at[yy], q.lc.at[1, own_slot], (i, to), n_lb)

            @pl.when(to == s)
            def _():
                keep(q.lat_in.at[yy], q.lc.at[0, own_slot], n_la)
                keep(q.cot_in.at[yy], q.lc.at[1, own_slot], n_lb)

    def media_share():
        arrive(q.media.at[pl.ds(0, z.ny)], n_ma)
        for t in range(1, z.ny):
            yy = (y + t) % z.ny
            send(q.media.at[yy * 2 + c], q.media.at[yy * 2 + c], sib, n_mb)

    def rows_sent():
        for yy in range(z.ny):
            @pl.when(yy * 2 + s // z.ny != s)
            def _():
                gone(q.lc.at[0, 0], n_la)
                gone(q.lc.at[0, 0], n_lb)
        if z.ny > 1:
            gone(q.media.at[pl.ds(0, z.ny - 1)], n_ma)
        gone(q.media.at[pl.ds(0, z.ny)], n_mb)

    def gather_start(buf, value, n):
        buf[pos] = value
        for t in range(1, TP):
            send(buf.at[pos], buf.at[pos], peer(t), n)

    def gather_end(buf, n):
        arrive(buf.at[pl.ds(0, TP - 1)], n)
        sent(buf.at[pl.ds(0, TP - 1)], n)

    def swap(ref, value, n):
        ref[...] = value
        send(ref, ref, sib, n)
        arrive(ref, n)
        sent(ref, n)

    def scatter_put(part, j):
        q.psend[j] = part.astype(BF).reshape(TP, z.r, z.d)

    def scatter_start(j):
        for t in range(1, TP):
            o = (pos + t) % TP
            send(q.psend.at[j, o], q.precv.at[j, pos], peer(t), n_rs[j])
        q.precv[j, pos] = q.psend[j, pos]

    def scatter_end(j):
        arrive(q.precv.at[j, pl.ds(0, TP - 1)], n_rs[j])
        sent(q.precv.at[j, pl.ds(0, TP - 1)], n_rs[j])
        out = q.precv[j, 0].astype(F32)
        for t in range(1, TP):
            out = out + q.precv[j, t].astype(F32)
        return out

    def vec(l, m):
        return q.nrm[6 * l + m][None, :]

    lane_head = lax.broadcasted_iota(jnp.int32, (1, H), 1) // HEAD

    def stack_heads(v):
        return jnp.concatenate([jnp.where(lane_head == h, v, jnp.zeros_like(v)) for h in range(z.heads)], axis=0)

    def fold_heads(v):
        out = None
        q.fold[...] = v
        for h in range(z.heads):
            part = jnp.where(lane_head == h, q.fold[h * z.latn:(h + 1) * z.latn], 0.0)
            out = part if out is None else out + part
        return out

    key_pos = lax.broadcasted_iota(jnp.int32, (1, z.keys), 1)
    live = (key_pos < q.counts[y]) | (key_pos >= z.pm)

    def norm_piece(j, _):
        xhat, _ = centre(q.media[j].astype(F32))
        rows = pl.ds(pl.multiple_of(j * z.pr, 8), z.pr)
        for l in range(L):
            q.mn[l, rows] = (xhat * vec(l, 0) + vec(l, 1)).astype(BF)
        return 0

    def media_kv(l):
        weights_end(l, "k")
        q.kv[l, :z.pm, :H] = dot(q.mn[l, :z.pm], w_k(l)).astype(BF)
        weights_end(l, "v")
        q.kv[l, :z.pm, H:] = dot(q.mn[l, :z.pm], w_v(l)).astype(BF)

    def attention(l):
        xhat, _ = centre(q.xs[l])
        swap(q.mn.at[l, at16(z.pm + c * z.r, z.r)], (xhat * vec(l, 2) + vec(l, 3)).astype(BF), n_ln[l])
        q.kv[l, z.pm:, :H] = dot(q.mn[l, z.pm:], w_k(l)).astype(BF)
        q.kv[l, z.pm:, H:] = dot(q.mn[l, z.pm:], w_v(l)).astype(BF)
        weights_end(l, "q")
        queries = stack_heads(dot(q.mn[l, z.pm:], w_q(l)).astype(BF))
        q.q4[l] = queries
        scores = dot(queries, q.kv[l, :, :H], 1, 1) * 0.125
        scores = jnp.where(live, scores, -1000000000.0)
        e = jnp.exp(scores - jnp.max(scores, axis=-1, keepdims=True))
        rt = jnp.sum(e, axis=-1, keepdims=True)
        q.pexp[l] = e
        q.rtot[l] = rt

    def attention_mix(l):
        own = fold_heads(dot(q.pexp[l].astype(BF), q.kv[l, :, H:]) / q.rtot[l])
        q.att4[l] = own
        swap(q.atta.at[l, c], own.astype(BF), n_at[l])

    def attention_out(l):
        mine = at16(c * z.r, z.r)
        att = jnp.concatenate([q.atta[l, 0, mine], q.atta[l, 1, mine]], axis=1)
        after = q.xs[l] + dot(att, q.wo[l].reshape(z.inner, z.d))
        q.aft[l] = after
        xhat, _ = centre(after)
        gather_start(q.ffa.at[l], (xhat * vec(l, 4) + vec(l, 5)).astype(BF), n_ff[l])

    def hidden(l):
        h = dot(q.ffa[l].reshape(z.rows, z.d), w_up(l))
        q.hp[l] = h
        q.act[l] = (h * (0.5 * (1.0 + lax.erf(h * 0.7071067811865476)))).astype(BF)

    def down(l):
        scatter_put(dot(q.act[l], w_dn(l)), l)

    def ff_back(l):
        g = dot(q.gza[l].reshape(z.rows, z.d), w_dn(l), 1, 1)
        h = q.hp[l]
        slope = 0.5 * (1.0 + lax.erf(h * 0.7071067811865476)) + h * 0.3989422804014327 * jnp.exp(-0.5 * h * h)
        q.gpre[l] = (g * slope).astype(BF)
        scatter_put(dot(q.gpre[l], w_up(l), 1, 1), L + l)
        scatter_start(L + l)

    def ff_grads(l):
        q.gdn[l] = dot(q.act[l], q.gza[l].reshape(z.rows, z.d), 0, 0).astype(BF).reshape(q.gdn.shape[1:])
        q.gup[l] = dot(q.ffa[l].reshape(z.rows, z.d), q.gpre[l], 0, 0).astype(BF).reshape(q.gup.shape[1:])

    def attn_back(l, gx):
        gff = scatter_end(L + l)
        xhat, rstd = centre(q.aft[l])
        q.gn[6 * l + 4] = jnp.sum(gff * xhat, axis=0)
        q.gn[6 * l + 5] = jnp.sum(gff, axis=0)
        gafter = gx + pull(xhat, rstd, gff, vec(l, 4))
        swap(q.gya.at[l, c], gafter.astype(BF), n_gy[l])
        out_grads(l)
        grads_first(l, "o")
        return gafter

    def attn_back_end(l, gafter):
        gy = q.gya[l].reshape(z.latn, z.d)
        hb = z.blk[0] // 2
        wo_own = q.wo[l, pl.ds(c * hb, hb)].reshape(H, z.d)
        gatt = dot(gy, wo_own, 1, 1).astype(BF)
        g4 = stack_heads(gatt.astype(F32))
        delta = jnp.sum(g4 * stack_heads(q.att4[l]), axis=-1, keepdims=True)
        rt = q.rtot[l]
        e = q.pexp[l]
        gp = dot(g4.astype(BF), q.kv[l, :, H:], 1, 1)
        gs = (e / rt * (gp - delta)).astype(BF)
        gq = (fold_heads(dot(gs, q.kv[l, :, :H])) * 0.125).astype(BF)
        gk = (dot(gs, q.q4[l], 0, 0) * 0.125).astype(BF)
        gv = dot(e.astype(BF), (g4 / rt).astype(BF), 0, 0).astype(BF)
        glat = jnp.concatenate([gq, gk[z.pm:], gv[z.pm:]], axis=1)
        w = jnp.concatenate([w_q(l), w_k(l), w_v(l)], axis=1)
        q.gl[l] = dot(glat, w, 1, 1).reshape(2, z.r, z.d)
        send(q.gl.at[l, 1 - c], q.grecv.at[l], sib, n_gl[l])
        q.gkvm[l, :, :H] = gk
        q.gkvm[l, :, H:] = gv
        arrive(q.grecv.at[l], n_gl[l])
        sent(q.grecv.at[l], n_gl[l])
        gln = q.gl[l, c] + q.grecv[l]
        xhat, rstd = centre(q.xs[l])
        q.gn[6 * l + 2] = jnp.sum(gln * xhat, axis=0)
        q.gn[6 * l + 3] = jnp.sum(gln, axis=0)
        return gafter + pull(xhat, rstd, gln, vec(l, 2)), gq

    def out_grads(l):
        att = jnp.concatenate([q.atta[l, 0], q.atta[l, 1]], axis=1)
        cols = lanes(c * (z.d // 2), z.d // 2)
        gyc = jnp.concatenate([q.gya[l, 0, :, cols], q.gya[l, 1, :, cols]], axis=0)
        g = dot(att, gyc, 0, 0).astype(BF).reshape(*z.blk, z.orows, z.d // 2)
        q.gao[l, :, :, :, :z.orows] = g[..., :z.quart]
        q.gao[l, :, :, :, z.orows:] = g[..., z.quart:]

    def qkv_grads(l, gq, p):
        shape = (*z.blk, z.qrows, H)
        if p == "q":
            q.gaq[l] = dot(q.mn[l, z.pm:], gq, 0, 0).astype(BF).reshape(shape)
        elif p == "k":
            q.gak[l] = dot(q.mn[l], q.gkvm[l, :, :H], 0, 0).astype(BF).reshape(shape)
        else:
            q.gav[l] = dot(q.mn[l], q.gkvm[l, :, H:], 0, 0).astype(BF).reshape(shape)

    def media_back(l):
        q.cm[...] = dot(q.gkvm[l, :z.pm], jnp.concatenate([w_k(l), w_v(l)], axis=1), 1, 1)

        def piece(j, sums):
            rows = pl.ds(pl.multiple_of(j * z.pr, 8), z.pr)
            xhat, rstd = centre(q.media[j].astype(F32))
            cotm = q.cm[rows]
            add = cotm * vec(l, 0)
            q.macc[rows] = add if l == L - 1 else q.macc[rows] + add
            return sums[0] + col_sum(cotm * xhat), sums[1] + col_sum(cotm)

        zero = jnp.zeros((1, z.d), F32)
        u, v = lax.fori_loop(0, z.ns, piece, (zero, zero))
        q.gn[6 * l + 0] = u[0]
        q.gn[6 * l + 1] = v[0]

    if z.fused:
        n_ra, n_rb, n_rc, n_rf = ({p: [sem() for _ in range(L)] for p in "kvqo"} for _ in range(4))
        n_ud, n_us, n_dd, n_ds = ([sem() for _ in range(L)] for _ in range(4))
        n_nd, n_ns = sem(), sem()

        def add_to(dst, x, w):
            dst[...] = (x[...].astype(F32) + w[...].astype(F32)).astype(BF)

        def at(name, l):
            return getattr(q, name).at[l]

        def grads_first(l, p):
            g, ra = at("ga" + p, l), at("ra" + p, l)
            send_by_core(g.at[:, :, 1 - y], ra, g.at[:, 1 - b], ra, second, n_ra[p][l])

        def grads_second(l, p):
            g, ra, sa, rb = at("ga" + p, l), at("ra" + p, l), at("sa" + p, l), at("rb" + p, l)
            arrive(ra, n_ra[p][l])
            sent(ra, n_ra[p][l])

            @pl.when(c == 0)
            def _():
                add_to(sa, g.at[:, :, y], ra)

            @pl.when(c == 1)
            def _():
                add_to(sa, g.at[:, b], ra)

            send_by_core(sa.at[:, 1 - b], rb, sa.at[:, 1 - y], rb, first, n_rb[p][l])

        def grads_third(l, p):
            sa, rb, sb, rc = at("sa" + p, l), at("rb" + p, l), at("sb" + p, l), at("rc" + p, l)
            arrive(rb, n_rb[p][l])
            sent(rb, n_rb[p][l])
            add_to(sb, sa.at[:, b * (1 - c) + y * c], rb)
            for t in range(1, za):
                o = (a + t) % za
                send(sb.at[o], rc.at[a], (o * 2 + b, s), n_rc[p][l])
            rc[a] = sb[a]

        def grads_last(l, p):
            rc, sf = at("rc" + p, l), at("sf" + p, l)
            part = rc.at[pl.ds(0, za - 1)]
            arrive(part, n_rc[p][l])
            sent(part, n_rc[p][l])
            v = rc[0].astype(F32)
            for t in range(1, za):
                v = v + rc[t].astype(F32)
            sf[...] = v
            if p != "o":
                mine, other = sf.at[at16(c * z.rq, z.rq)], sf.at[at16((1 - c) * z.rq, z.rq)]
                out = q.qs_out.at[l, "qkv".index(p), c]
                keep(mine, out, n_rf[p][l])
                send(other, out, sib, n_rf[p][l])
            else:
                for h in range(2):
                    mine, other = (sf.at[at16(h * z.orows + cc * z.ro, z.ro)] for cc in (c, 1 - c))
                    keep(mine, q.os_out.at[l, c, h], n_rf[p][l])
                    send(other, q.os_out.at[l, c, h], sib, n_rf[p][l])

        def grads_out(l, p):
            out = q.os_out.at[l] if p == "o" else q.qs_out.at[l, "qkv".index(p)]
            arrive(out, n_rf[p][l])
            sent(out.at[0], n_rf[p][l])

        def ff_pair(l):
            send(q.gup.at[l, :, 1 - c], q.updr.at[l], sib, n_ud[l])
            send(q.gdn.at[l, :, 1 - c], q.dndr.at[l], sib, n_dd[l])

        def ff_spread(l):
            arrive(q.dndr.at[l], n_dd[l])
            sent(q.dndr.at[l], n_dd[l])
            add_to(q.dns.at[l], q.gdn.at[l, :, c], q.dndr.at[l])
            for g in range(1, z.dp):
                o = (grp + g) % z.dp
                send(q.dns.at[l, o], q.dnr.at[l, grp], chip(o * TP + pos, c), n_ds[l])
            arrive(q.updr.at[l], n_ud[l])
            sent(q.updr.at[l], n_ud[l])
            add_to(q.ups.at[l], q.gup.at[l, :, c], q.updr.at[l])

            def one(t, _):
                kk = (k + t) % z.chips
                send(q.ups.at[l, kk], q.upr.at[l, k], chip(kk, c), n_us[l])
                return 0

            lax.fori_loop(1, z.chips, one, 0)
            keep(q.dns.at[l, grp], q.dnr.at[l, grp], n_ds[l])
            keep(q.ups.at[l, k], q.upr.at[l, k], n_us[l])

        def ff_out(l):
            arrive(q.dnr.at[l], n_ds[l])
            sent(q.dns.at[l, pl.ds(0, z.dp - 1)], n_ds[l])
            arrive(q.upr.at[l], n_us[l])
            sent(q.ups.at[l, pl.ds(0, z.chips - 1)], n_us[l])

        def norms_pair():
            send(q.gn, q.gnd, sib, n_nd)

        def norms_spread():
            arrive(q.gnd, n_nd)
            sent(q.gnd, n_nd)
            q.gns[...] = q.gn[...] + q.gnd[...]

            def one(t, _):
                kk = (k + t) % z.chips
                dev = chip(kk, c)
                send(q.gns.at[:, lanes(dev[0] * z.lanes, z.lanes)], q.gnr.at[k], dev, n_ns)
                return 0

            lax.fori_loop(1, z.chips, one, 0)
            keep(q.gns.at[:, lanes(i * z.lanes, z.lanes)], q.gnr.at[k], n_ns)

        def norms_out():
            arrive(q.gnr, n_ns)
            sent(q.gnr.at[pl.ds(0, z.chips - 1)], n_ns)
    else:
        def grads_first(l, p):
            n = 11 + "kvqo".index(p) * L + l
            pltpu.make_async_copy(getattr(q, "ga" + p).at[l], getattr(q, f"ga{p}_out").at[l], ls.at[n]).start()

        def grads_out(l, p):
            n = 11 + "kvqo".index(p) * L + l
            pltpu.make_async_copy(getattr(q, "ga" + p).at[l], getattr(q, f"ga{p}_out").at[l], ls.at[n]).wait()

        def ff_pair(l):
            pltpu.make_async_copy(q.gup.at[l], q.gup_out.at[l], ls.at[19 + l]).start()
            pltpu.make_async_copy(q.gdn.at[l], q.gdn_out.at[l], ls.at[21 + l]).start()

        def ff_out(l):
            pltpu.make_async_copy(q.gup.at[l], q.gup_out.at[l], ls.at[19 + l]).wait()
            pltpu.make_async_copy(q.gdn.at[l], q.gdn_out.at[l], ls.at[21 + l]).wait()

        grads_second = grads_third = grads_last = ff_spread = nothing

        def norms_pair():
            pass

        def norms_spread():
            pass

        def norms_out():
            pltpu.make_async_copy(q.gn, q.gn_out, ls.at[23]).start()
            pltpu.make_async_copy(q.gn, q.gn_out, ls.at[23]).wait()

    weights_pair(0)
    norms_start()
    rows_start()
    weights_z(0, "k")
    weights_z(0, "v")
    weights_z(0, "q")
    weights_z(0, "o")
    norms_spread_in()
    for l in range(1, L):
        weights_pair(l)
    weights_first(0, "k")
    arrive(q.lc.at[0], n_la)
    q.xs[0] = q.lc[0].astype(F32).reshape(z.r, z.d)
    media_share()
    weights_first(0, "v")
    norms_end()
    weights_second(0, "k")
    weights_first(0, "q")
    arrive(q.media.at[pl.ds(0, z.ny)], n_mb)
    weights_second(0, "v")
    weights_first(0, "o")
    for l in range(1, L):
        weights_z(l, "kvqo")
    weights_ff(0)
    lax.fori_loop(0, z.ns // 2, norm_piece, 0)
    weights_second(0, "q")
    lax.fori_loop(z.ns // 2, z.ns, norm_piece, 0)
    weights_second(0, "o")
    arrive(q.lc.at[1], n_lb)
    cot = q.lc[1].astype(F32).reshape(z.r, z.d)
    media_kv(0)
    for l in range(L):
        attention(l)
        if l + 1 < L:
            weights_first(l + 1, "kvqo")
        else:
            gather_start(q.gza.at[l], cot.astype(BF), n_gz[l])
        attention_mix(l)
        weights_end(l, "o")
        weights_out_end(l)
        attention_out(l)
        if l + 1 < L:
            weights_second(l + 1, "kvqo")
        weights_ff_share(l)
        weights_ff_end(l)
        if l + 1 < L:
            weights_ff(l + 1)
        gather_end(q.ffa.at[l], n_ff[l])
        hidden(l)
        if l + 1 < L:
            down(l)
            scatter_start(l)
            media_kv(l + 1)
            q.xs[l + 1] = q.aft[l] + scatter_end(l)
    gx = cot
    for l in reversed(range(L)):
        if l < L - 1:
            gather_start(q.gza.at[l], gx.astype(BF), n_gz[l])
            qkv_grads(l + 1, gq, "k")
            grads_first(l + 1, "k")
            grads_second(l + 1, "o")
            qkv_grads(l + 1, gq, "v")
            qkv_grads(l + 1, gq, "q")
            media_back(l + 1)
        gather_end(q.gza.at[l], n_gz[l])
        ff_back(l)
        if l < L - 1:
            grads_first(l + 1, "v")
            grads_first(l + 1, "q")
        ff_grads(l)
        ff_pair(l)
        if l < L - 1:
            grads_second(l + 1, "k")
            grads_third(l + 1, "o")
        else:
            down(l)
        ff_spread(l)
        gafter = attn_back(l, gx)
        if l < L - 1:
            grads_second(l + 1, "v")
            grads_second(l + 1, "q")
            grads_third(l + 1, "k")
        else:
            scatter_start(l)
        gx, gq = attn_back_end(l, gafter)
    qkv_grads(0, gq, "k")
    grads_first(0, "k")
    qkv_grads(0, gq, "v")
    grads_first(0, "v")
    qkv_grads(0, gq, "q")
    grads_first(0, "q")
    grads_second(0, "o")
    for l in range(1, L):
        grads_third(l, "v")
        grads_third(l, "q")
        grads_last(l, "o")
        grads_last(l, "k")
    q.gxo[...] = gx.reshape(z.ny, z.lr, z.d)
    q.xout[...] = (q.aft[L - 1] + scatter_end(L - 1)).astype(z.lt).reshape(z.ny, z.lr, z.d)

    def give_back(srcs, out, n):
        for j in range(z.ny):
            to = c * z.ny + j

            @pl.when(to != s)
            def _():
                send(srcs[j], out.at[y], (i, to), n)

            @pl.when(to == s)
            def _():
                keep(srcs[j], out.at[y], n)

    give_back([q.xout.at[j] for j in range(z.ny)], q.lat_out, n_lo)
    give_back([q.gxo.at[j] for j in range(z.ny)], q.glat_out, n_go)
    media_back(0)
    norms_pair()
    h = z.pm // 2
    q.msend[...] = q.macc[at16((1 - c) * h, h)].astype(z.mt)
    send(q.msend, q.mrecv, sib, n_md)
    grads_second(0, "k")
    grads_second(0, "v")
    grads_second(0, "q")
    grads_third(0, "o")
    norms_spread()
    arrive(q.mrecv, n_md)
    sent(q.mrecv, n_md)
    xhat, rstd = centre(q.media[pl.ds(c * z.ny, z.ny)].astype(F32).reshape(h, z.d))
    gm = pull(xhat, rstd, q.macc[at16(c * h, h)] + q.mrecv[...].astype(F32), jnp.ones((1, z.d), F32))
    mo = q.mn.at[0] if z.mt == BF else q.cm
    for j in range(z.ny):
        mo[j * z.pr:(j + 1) * z.pr] = gm[j * z.pr:(j + 1) * z.pr].astype(z.mt)
    srcs = [mo.at[pl.ds(j * z.pr, z.pr)] for j in range(z.ny)]
    give_back(srcs, q.gmedia_out, n_mo)
    grads_third(0, "k")
    grads_third(0, "v")
    grads_third(0, "q")
    for l in range(1, L):
        grads_last(l, "v")
        grads_last(l, "q")
    grads_last(0, "o")
    for l in range(1, L):
        grads_out(l, "o")
        grads_out(l, "k")
        grads_out(l, "v")
        grads_out(l, "q")
        ff_out(l)
    ff_out(0)
    norms_out()
    grads_last(0, "k")
    grads_last(0, "v")
    grads_last(0, "q")
    grads_out(0, "o")
    grads_out(0, "k")
    grads_out(0, "v")
    grads_out(0, "q")
    arrive(q.lat_out, n_lo)
    arrive(q.glat_out, n_go)
    arrive(q.gmedia_out, n_mo)
    rows_sent()
    for j in range(z.ny):
        @pl.when(c * z.ny + j != s)
        def _():
            gone(q.xout.at[0], n_lo)
            gone(q.gxo.at[0], n_go)
            gone(srcs[0], n_mo)
    for ref, n in waits:
        gone(ref, n)


def call(z, *args):
    ins, outs, scratch = inputs_of(z), outputs_of(z), scratch_of(z)
    names = [n for n, _ in ins] + list(outs) + list(scratch)
    got = pl.pallas_call(
        functools.partial(kernel, z, names),
        out_shape=[jax.ShapeDtypeStruct(s, d) for s, d in outs.values()],
        in_specs=[pl.BlockSpec(memory_space=m) for _, m in ins],
        out_specs=[pl.BlockSpec(memory_space=pl.ANY)] * len(outs),
        scratch_shapes=list(scratch.values()),
        compiler_params=pltpu.CompilerParams(collective_id=0, has_side_effects=True, vmem_limit_bytes=62 * 2**20),
    )(*args)
    return types.SimpleNamespace(**dict(zip(outs, got)))


def finish_kernel(z, lat_in, gm_in, gl_in, qs, os, upr, dnr, gnr, lat, gm, gl, gq, gkv, go, gup, gdn, gn):
    H = z.half
    lat[...] = lat_in[...]
    gm[...] = gm_in[...].astype(F32)
    gl[...] = gl_in[...]
    for cc in range(2):
        gq[0, :, cc * H:(cc + 1) * H] = qs[0, 0, cc]
        gkv[0, :, cc * H:(cc + 1) * H] = qs[0, 1, cc]
        gkv[0, :, z.inner + cc * H:z.inner + (cc + 1) * H] = qs[0, 2, cc]
        for h in range(2):
            col = cc * (z.d // 2) + h * z.quart
            go[0, :, col:col + z.quart] = os[0, cc, h]
    v = dnr[0, 0].astype(F32)
    for g in range(1, z.dp):
        v = v + dnr[0, g].astype(F32)
    gdn[0] = v
    for p in range(TP):
        v = upr[0, p].astype(F32)
        for g in range(1, z.dp):
            v = v + upr[0, g * TP + p].astype(F32)
        for g in range(z.dp):
            col = (g * TP + p) * z.fc
            gup[0, :, col:col + z.fc] = v[:, g * z.fc:(g + 1) * z.fc]
    s = lax.axis_index("seq")
    width = z.lanes // z.ns
    v = gnr[0]
    for t in range(1, z.chips):
        v = v + gnr[t]
    mine = v[:, :width]
    for j in range(1, z.ns):
        mine = jnp.where(s == j, v[:, j * width:(j + 1) * width], mine)
    for l in range(z.layers):
        gn[l] = mine[6 * l:6 * l + 6]


def finish(z, o):
    L, D = z.layers, z.d
    step = lambda *shape: pl.BlockSpec((1, *shape), lambda n: (n,) + (0,) * len(shape))
    whole = lambda *shape: pl.BlockSpec(shape, lambda n: (0,) * len(shape))
    width = z.lanes // z.ns
    outs = [
        ((z.ny, z.lr, D), BF), ((z.ny, z.pr, D), F32), ((z.ny, z.lr, D), F32), ((L, z.rq, z.inner), F32),
        ((L, z.rq, 2 * z.inner), F32), ((L, z.ro, D), F32), ((L, z.rq, z.ff), F32), ((L, z.rd, D), F32),
        ((L, 6, width), F32),
    ]
    return pl.pallas_call(
        functools.partial(finish_kernel, z),
        grid=(L,),
        out_shape=[jax.ShapeDtypeStruct(s, d) for s, d in outs],
        in_specs=[
            step(z.lr, D), step(z.pr, D), step(z.lr, D), step(3, 2, z.rq, z.half), step(2, 2, z.ro, z.quart),
            step(z.chips, z.rq, z.fs), step(z.dp, z.rd, D), whole(z.chips, 16, z.lanes),
        ],
        out_specs=[step(*s[1:]) for s, _ in outs[:-1]] + [whole(L, 6, width)],
        compiler_params=pltpu.CompilerParams(vmem_limit_bytes=62 * 2**20),
    )(o.lat_out, o.gmedia_out, o.glat_out, o.qs_out, o.os_out, o.upr, o.dnr, o.gnr)


def body(mesh, media, latents, counts, wq, wkv, wout, wup, wdown, norms, cotangent):
    z = Sizes(mesh, media, latents, wq, wkv, wout, wup, wdown)
    L, D, H = z.layers, z.d, z.half
    i, s = lax.axis_index("img"), lax.axis_index("seq")
    y, c = s // 2, s % 2
    k = i * z.ny + y
    pos = k % TP
    media, latents, cotangent = media.astype(z.mt), latents.astype(z.lt), cotangent.astype(z.lt)
    own = norms.reshape(6 * L, -1)
    if z.fused:
        width = own.shape[1]
        tile = jnp.zeros((16, z.lanes), own.dtype)
        tile = lax.dynamic_update_slice(tile, own, (0, s * width))
        o = call(z, media, latents, cotangent, counts, tile, wq, wkv, wout, wup, wdown)
        return tuple(finish(z, o))

    def pick(v, axis, index):
        return lax.dynamic_index_in_dim(v, index, axis, keepdims=False)

    def gather(v, axis):
        return lax.all_gather(v, BOTH, axis=axis, tiled=True)

    nrm = jnp.pad(gather(own, 1).astype(F32), ((0, 16 - 6 * L), (0, 0)))
    fq = pick(gather(wq, 1).reshape(L, D, 2, H), 2, c)
    fkv = pick(gather(wkv, 1).reshape(L, D, 2, 2, H), 3, c).reshape(L, D, 2 * H)
    fq = fq.reshape(L, *z.blk, z.qrows, H)
    fk, fv = (fkv[:, :, n * H:(n + 1) * H].reshape(L, *z.blk, z.qrows, H) for n in range(2))
    wo = gather(wout, 1).reshape(L, *z.blk, 2, z.orows // 2, D)
    fup = pick(gather(wup, 1).reshape(L, D, z.dp, TP, z.fc), 3, pos).reshape(L, 1, 2, D // 2, z.fs)
    fdn = pick(gather(wdown, 1).reshape(L, z.dp, TP, z.fc, D), 2, pos).reshape(L, 1, 2, z.fs // 2, D)
    o = call(z, media, latents, cotangent, counts, nrm, fq, fk, fv, wo, fup, fdn)

    def spread(g, shape, axis, index):
        return lax.dynamic_update_index_in_dim(jnp.zeros(shape, F32), g.astype(F32), index, axis)

    def scatter(g):
        return lax.psum_scatter(g, BOTH, scatter_dimension=1, tiled=True)

    gao = o.gao_out.reshape(L, z.nblk, 2, z.orows, z.quart)
    gout = jnp.concatenate([gao[:, :, 0], gao[:, :, 1]], axis=3).reshape(L, z.inner, D // 2)
    gat = jnp.concatenate([v.reshape(L, D, H) for v in (o.gaq_out, o.gak_out, o.gav_out)], axis=2)
    gq = scatter(spread(gat[:, :, :H], (L, D, 2, H), 2, c).reshape(L, D, z.inner))
    gkv = spread(gat[:, :, H : 3 * H].reshape(L, D, 2, H), (L, D, 2, 2, H), 3, c)
    gkv = scatter(gkv.reshape(L, D, 2 * z.inner))
    go = scatter(spread(gout, (L, z.inner, 2, D // 2), 2, c).reshape(L, z.inner, D))
    gu = spread(o.gup_out.reshape(L, D, z.dp, z.fc), (L, D, z.dp, TP, z.fc), 3, pos)
    gu = scatter(gu.reshape(L, D, z.ff))
    gd = spread(o.gdn_out.reshape(L, z.dp, z.fc, D), (L, z.dp, TP, z.fc, D), 2, pos)
    gd = scatter(gd.reshape(L, z.ff, D))
    gn = lax.psum_scatter(o.gn_out, BOTH, scatter_dimension=1, tiled=True)[: 6 * L].reshape(L, 6, -1)
    return o.lat_out.astype(BF), o.gmedia_out.astype(F32), o.glat_out, gq, gkv, go, gu, gd, gn


def solution(mesh):
    rows = P("img", "seq", None)
    weight = P(None, BOTH, None)
    return jax.shard_map(
        functools.partial(body, mesh),
        mesh=mesh,
        in_specs=(rows, rows, P("img"), weight, weight, weight, weight, weight, P(None, None, BOTH), rows),
        out_specs=(rows, rows, rows, weight, weight, weight, weight, weight, P(None, None, BOTH)),
        check_vma=False,
    )
```

time: 219 us -> 199 us (0.909); the launches traced: 219 us -> 196 us
  Pallas kernels: 206 us -> 192 us
  local copies, waits for them, and re-layouts: 8.03 us -> 3.21 us
  other arithmetic: 3.86 us -> 0 us
    pallas_call x1, Pallas kernels: 206 us -> 189 us  [call(): pl.pallas_call(functools.partial(kernel, z, names), out_shape=[jax.ShapeD...]
    unnamed x25 -> x3, local copies, waits for them, and re-layouts: 6.56 us -> 1.28 us
    pallas_call x0 -> x1, Pallas kernels: none -> 3.99 us  [finish(): pl.pallas_call(functools.partial(finish_kernel, z), grid=(L,), out_shape=...]
    convert_element_type x1 -> x0, other arithmetic: 2.32 us -> none  [body(): o.gmedia_out.astype(F32)]
where the time goes in v3:
time: 199 us; the launch traced here: 196 us
  Pallas kernels  192 us (96%)
  local copies, waits for them, and re-layouts  3.21 us (2%)
    pallas_call x1, Pallas kernels, call(): pl.pallas_call(functools.partial(kernel, z, names), out_shape=[jax.ShapeD...  189 us
    pallas_call x1, Pallas kernels, finish(): pl.pallas_call(functools.partial(finish_kernel, z), grid=(L,), out_shape=...  3.99 us

profile of v3, /device:TPU:9, one launch (start us, length us, event | category | flops | bytes accessed | tf_op | source)
XLA Modules:
  0.0 196.4 jit_solution(16215373783019116801)
XLA Ops:
  0.6 0.7 copy.21
  1.4 0.6 dynamic_update_slice.3.refs_4_
  2.0 0.0 copy-start
  2.0 0.6 copy-done
  2.6 188.5 %shard_map.169 = (bf16[2,16,1024]{2,1,0:T(8,128)(2,1)}, bf16[2,144,1024]{2,1,0:T(8,128)(2,1)}, f32[2,16,1024]{2,1,0:T(8,128)}, f32[2,3,2,32,256]{4,3,2,1,0:T(8,1...) custom-call(bf16[2,144,1024]{2,1,0:T(8,128)(2,1)} %refs_0_.1, ...), custom_call_target="tpu_custom_call" | custom-call | tf_op jit(solution)/shard_map/pallas_call | solution.py:984
  191.1 4.0 %shard_map.170 = (bf16[2,16,1024]{2,1,0:T(8,128)(2,1)}, f32[2,144,1024]{2,1,0:T(8,128)}, f32[2,16,1024]{2,1,0:T(8,128)}, f32[2,32,512]{2,1,0:T(8,128)}, f32[2,32...) custom-call(bf16[2,16,1024]{2,1,0:T(8,128)(2,1)} %get-tuple-element., ...), custom_call_target="tpu_custom_call" | custom-call | tf_op jit(solution)/shard_map/pallas_call | solution.py:1040
  195.1 1.3 copy.22
  (2 shorter events, 0.0 us)
Async XLA Ops:
  2.0 0.6 copy-start

commit v4 on v3

--- a/solution.py
+++ b/solution.py
@@ -483,7 +483,7 @@
 
     def gather_start(buf, value, n):
         buf[pos] = value
-        for t in range(1, TP):
+        for t in [3, 5, 6, 7, 1, 2, 4]:
             send(buf.at[pos], buf.at[pos], peer(t), n)
 
     def gather_end(buf, n):
@@ -500,7 +500,7 @@
         q.psend[j] = part.astype(BF).reshape(TP, z.r, z.d)
 
     def scatter_start(j):
-        for t in range(1, TP):
+        for t in [3, 5, 6, 7, 1, 2, 4]:
             o = (pos + t) % TP
             send(q.psend.at[j, o], q.precv.at[j, pos], peer(t), n_rs[j])
         q.precv[j, pos] = q.psend[j, pos]
@@ -832,9 +832,9 @@
     weights_first(0, "o")
     for l in range(1, L):
         weights_z(l, "kvqo")
-    weights_ff(0)
     lax.fori_loop(0, z.ns // 2, norm_piece, 0)
     weights_second(0, "q")
+    weights_ff(0)
     lax.fori_loop(z.ns // 2, z.ns, norm_piece, 0)
     weights_second(0, "o")
     arrive(q.lc.at[1], n_lb)
@@ -846,8 +846,8 @@
             weights_first(l + 1, "kvqo")
         else:
             gather_start(q.gza.at[l], cot.astype(BF), n_gz[l])
+        weights_end(l, "o")
         attention_mix(l)
-        weights_end(l, "o")
         weights_out_end(l)
         attention_out(l)
         if l + 1 < L:
@@ -885,14 +885,13 @@
             grads_third(l + 1, "o")
         else:
             down(l)
+            scatter_start(l)
         ff_spread(l)
         gafter = attn_back(l, gx)
         if l < L - 1:
             grads_second(l + 1, "v")
             grads_second(l + 1, "q")
             grads_third(l + 1, "k")
-        else:
-            scatter_start(l)
         gx, gq = attn_back_end(l, gafter)
     qkv_grads(0, gq, "k")
     grads_first(0, "k")

time: 199 us -> 196 us (0.985)
  no operation moved by 1% of the time
where the time goes in v4:
time: 196 us; the launch traced here: 195 us
  Pallas kernels  191 us (97%)
  local copies, waits for them, and re-layouts  3.21 us (2%)
    pallas_call x1, Pallas kernels, call(): pl.pallas_call(functools.partial(kernel, z, names), out_shape=[jax.ShapeD...  187 us
    pallas_call x1, Pallas kernels, finish(): pl.pallas_call(functools.partial(finish_kernel, z), grid=(L,), out_shape=...  3.99 us

profile of v4, /device:TPU:9, one launch (start us, length us, event | category | flops | bytes accessed | tf_op | source)
XLA Modules:
  0.0 194.7 jit_solution(14946849489149547900)
XLA Ops:
  0.6 0.7 copy.21
  1.4 0.6 dynamic_update_slice.3.refs_4_
  2.0 0.0 copy-start
  2.0 0.6 copy-done
  2.6 186.8 %shard_map.169 = (bf16[2,16,1024]{2,1,0:T(8,128)(2,1)}, bf16[2,144,1024]{2,1,0:T(8,128)(2,1)}, f32[2,16,1024]{2,1,0:T(8,128)}, f32[2,3,2,32,256]{4,3,2,1,0:T(8,1...) custom-call(bf16[2,144,1024]{2,1,0:T(8,128)(2,1)} %refs_0_.1, ...), custom_call_target="tpu_custom_call" | custom-call | tf_op jit(solution)/shard_map/pallas_call | solution.py:983
  189.4 4.0 %shard_map.170 = (bf16[2,16,1024]{2,1,0:T(8,128)(2,1)}, f32[2,144,1024]{2,1,0:T(8,128)}, f32[2,16,1024]{2,1,0:T(8,128)}, f32[2,32,512]{2,1,0:T(8,128)}, f32[2,32...) custom-call(bf16[2,16,1024]{2,1,0:T(8,128)(2,1)} %get-tuple-element., ...), custom_call_target="tpu_custom_call" | custom-call | tf_op jit(solution)/shard_map/pallas_call | solution.py:1039
  193.4 1.3 copy.22
  (2 shorter events, 0.0 us)
Async XLA Ops:
  2.0 0.6 copy-start
